TPU v7x, 512 devices: a whole 4x8x8 slice. The times are simulated.
512 devices in a mesh: ctx: 16 (over y_lo, x), ch: 32 (over z, y_hi, core).
Axes of the slice: x: 4, y: 8 (y_hi: 2, y_lo: 4; y = y_hi * 4 + y_lo), z: 8, core: 2. Of those that a mesh axis runs over, the one named last changes fastest.
Arguments:
- conv_input: bfloat16 [4096, 8192], P('ctx', 'ch'), may hold values from -6 to 6
- gate: bfloat16 [4096, 8192], P('ctx', 'ch'), may hold values from -6 to 6
- out_grad: bfloat16 [4096, 8192], P('ctx', 'ch'), may hold values from -6 to 6
- out_weight: bfloat16 [8192, 8192], P('ch'), may hold values from -0.0625 to 0.0625
- filter_taps: bfloat16 [4096, 8192], P('ctx', 'ch'), may hold values from -0.09375 to 0.09375
Outputs:
- input_grad: float32 [4096, 8192], P('ctx', 'ch')
- filter_grad: float32 [4096, 8192], P('ctx', 'ch')
All inputs are finite; a program needn't handle non-finite values.
Results may differ from a plain program's by a relative error of at most 0.0029.
Values may be sent and summed in bfloat16 or wider, within the bound.
No kernel may reach another device: no remote copies, remote signals or barrier semaphores. Data moves between devices by JAX's collectives and lax.ppermute only.
A program may use at most 128 MiB of HBM per device.

v0:
```python
import math

import jax
import jax.numpy as jnp
from jax import lax
from jax.sharding import PartitionSpec as P


def shifted(value, axis, steps):
    count = lax.axis_size(axis)
    leading, last = (max(0, -steps), min(count, count - steps))
    return lax.ppermute(value, axis, [(source, source + steps) for source in range(leading, last)])


def real_tables(slab_rows):
    period = 2 * slab_rows
    sample = jnp.arange(period, dtype=jnp.int32)
    freq = jnp.arange(slab_rows, dtype=jnp.int32)
    phase = freq[:, None] * sample[None, :] % period
    angle = phase.astype(jnp.float32) * (2.0 * math.pi / period)
    alternate = (1.0 - 2.0 * (sample % 2).astype(jnp.float32))[None, :]
    sine_rows = jnp.where(freq[:, None] == 0, alternate, -jnp.sin(angle))
    return jnp.concatenate([jnp.cos(angle), sine_rows], axis=0)


def shards(conv_input, gate, out_grad, out_weight, filter_taps):
    slab_rows = conv_input.shape[0]
    period = 2 * slab_rows
    group_size = lax.axis_size("ctx")
    channels = out_weight.shape[0]
    table = real_tables(slab_rows)
    freq = jnp.arange(slab_rows, dtype=jnp.int32)
    first = (freq == 0).astype(jnp.float32)[:, None]
    later = 1.0 - first
    sign_k = (1.0 - 2.0 * (freq % 2).astype(jnp.float32))[:, None]
    nyquist_sign = 1.0 - 2.0 * float(slab_rows % 2)
    weight = 2.0 - first
    low_factor = sign_k * weight / period
    high_factor = (later * sign_k + first * nyquist_sign) * weight / period

    def spectrum(values):
        return jnp.dot(
            table[:, : values.shape[0]],
            values.astype(jnp.float32),
            precision=lax.Precision.HIGHEST,
            preferred_element_type=jnp.float32,
        )

    def correlate(left, right):
        left_re, left_im = (left[:slab_rows], left[slab_rows:])
        right_re, right_im = (right[:slab_rows], right[slab_rows:])
        both_im = left_im * right_im
        real_part = left_re * right_re + later * both_im
        imag_part = later * (left_im * right_re - left_re * right_im) + first * both_im
        return jnp.concatenate([real_part * low_factor, imag_part * high_factor], axis=0)

    pre_gate = lax.dot_general(
        lax.all_gather(out_grad, "ch", axis=1, tiled=True),
        out_weight,
        (((1,), (1,)), ((), ())),
        preferred_element_type=jnp.float32,
    )
    gated = (gate.astype(jnp.float32) * pre_gate).astype(jnp.bfloat16)
    taps = lax.all_gather(filter_taps, "ctx", axis=0, tiled=True)
    padded = jnp.concatenate([jnp.zeros((slab_rows, channels), jnp.bfloat16), taps], axis=0)

    def filter_spectrum(lag_index):
        window = lax.dynamic_slice_in_dim(padded, lag_index * slab_rows, period, 0)
        return spectrum(window)

    input_spec = spectrum(conv_input)

    def visit(state, slab_grad, lag_index):
        total, lag_totals = state
        slab_spec = spectrum(slab_grad)
        total = total + correlate(slab_spec, filter_spectrum(lag_index))
        cross = correlate(slab_spec, input_spec)
        window = lax.dot_general(
            table,
            cross,
            (((0,), (0,)), ((), ())),
            precision=lax.Precision.HIGHEST,
            preferred_element_type=jnp.float32,
        )
        start = lag_index * slab_rows
        current = lax.dynamic_slice_in_dim(lag_totals, start, period, 0)
        lag_totals = lax.dynamic_update_slice_in_dim(lag_totals, current + window, start, 0)
        return (total, lag_totals)

    zero_spec = jnp.zeros((period, channels), jnp.float32)
    zero_lags = jnp.zeros(((group_size + 1) * slab_rows, channels), jnp.float32)
    state = visit((zero_spec, zero_lags), gated, 0)

    def step_one(lag_index, carry):
        state, moving = carry
        moving = shifted(moving, "ctx", -1)
        return (visit(state, moving, lag_index), moving)

    state, moving = lax.fori_loop(1, group_size, step_one, (state, gated))
    total, lag_totals = state
    input_grad = lax.dot_general(
        table[:, :slab_rows],
        total,
        (((0,), (0,)), ((), ())),
        precision=lax.Precision.HIGHEST,
        preferred_element_type=jnp.float32,
    )
    scaled = lag_totals[slab_rows:] * (1.0 / math.sqrt(group_size * slab_rows))
    filter_grad = lax.psum_scatter(scaled, "ctx", scatter_dimension=0, tiled=True)
    return (input_grad, filter_grad)


def solution(mesh):
    return jax.shard_map(
        shards,
        mesh=mesh,
        in_specs=(P("ctx", "ch"), P("ctx", "ch"), P("ctx", "ch"), P("ch", None), P("ctx", "ch")),
        out_specs=(P("ctx", "ch"), P("ctx", "ch")),
        check_vma=False,
    )
```

profile of v0, /device:TPU:64, one launch (start us, length us, event | category | flops | bytes accessed | tf_op | source)
XLA Modules:
  0.0 522.1 jit_solution(4302692637131834327)
XLA Ops:
  8.8 2.1 negate_select_fusion.2
  11.4 88.8 %all-gather.5.cloned.1.call-done = bf16[4096,256]{1,0:T(8,128)(2,1)} async-done(((bf16[256,256]{1,0:T(8,128)(2,1)}), bf16[4096,256]{1,0:T(8,128)(2,1)}) %all-gather.5.cloned.1.call-update) | async-done | bytes 2097168 | tf_op jit(solution)/shard_map/all_gather | solution.py:64
  100.2 3.3 concatenate.27
  104.8 103.6 %all-gather.3.cloned.1.call-done = bf16[256,8192]{1,0:T(8,128)(2,1)} async-done(((bf16[256,256]{1,0:T(8,128)(2,1)}), bf16[256,8192]{1,0:T(8,128)(2,1)}) %all-gather.3.cloned.1.call-update) | async-done | bytes 4194320 | tf_op jit(solution)/shard_map/all_gather | solution.py:58
  208.5 4.8 fusion.20
  216.8 2.3 dynamic_update_slice.10.clone2
  219.2 193.0 %while.19 = (s32[]{:T(128)}, f32[512,256]{1,0:T(8,128)}, f32[4352,256]{1,0:T(8,128)}, bf16[256,256]{1,0:T(8,128)(2,1)S(1)}, f32[512,512]{1,0:T(8,128)S(1)}, /*in...) while((s32[]{:T(128)}, f32[512,256]{1,0:T(8,128)}, ...), condition=%wide.region_1.2_spmd.clone.clone, body=%wide.region_0.1_spmd.clone.clone.sunk | while | flops 2015372288 | bytes 15347919 | solution.py:99
  223.4 3.3 collective-permute-done
  235.2 2.6 collective-permute-done
  246.3 2.6 collective-permute-done
  251.1 2.1 maximum_add_fusion.2
  257.5 3.2 collective-permute-done
  262.8 2.1 maximum_add_fusion.2
  269.2 4.6 collective-permute-done
  282.3 4.7 collective-permute-done
  295.5 4.7 collective-permute-done
  302.3 2.1 maximum_add_fusion.2
  308.7 4.7 collective-permute-done
  315.6 2.1 maximum_add_fusion.2
  322.0 4.7 collective-permute-done
  328.8 2.1 maximum_add_fusion.2
  335.2 4.7 collective-permute-done
  348.5 5.0 collective-permute-done
  362.0 6.4 %collective-permute-done = bf16[256,256]{1,0:T(8,128)(2,1)S(1)} collective-permute-done((bf16[256,256]{1,0:T(8,128)(2,1)S(1)}, bf16[256,256]{1,0:T(8,128)(2,1)S(1)}, u32[]{:S(2)}, u32[]{:S(2)}) %collective-permute-start) | collective-permute-done | bytes 131104 | tf_op jit(solution)/shard_map/while/body/eval_jaxpr/ppermute | solution.py:12
  370.5 2.1 maximum_add_fusion.2
  376.9 5.3 %collective-permute-done = bf16[256,256]{1,0:T(8,128)(2,1)S(1)} collective-permute-done((bf16[256,256]{1,0:T(8,128)(2,1)S(1)}, bf16[256,256]{1,0:T(8,128)(2,1)S(1)}, u32[]{:S(2)}, u32[]{:S(2)}) %collective-permute-start) | collective-permute-done | bytes 131104 | tf_op jit(solution)/shard_map/while/body/eval_jaxpr/ppermute | solution.py:12
  390.6 4.6 collective-permute-done
  397.3 2.1 maximum_add_fusion.2
  403.7 4.2 collective-permute-done
  410.0 2.1 maximum_add_fusion.2
  412.1 4.5 slice_multiply_fusion.2
  419.7 95.8 %reduce-scatter.2.cloned.1.call-done = f32[256,256]{1,0:T(8,128)} async-done(((f32[4096,256]{1,0:T(8,128)}), f32[256,256]{1,0:T(8,128)}) %reduce-scatter.2.cloned.1.call-update) | async-done | bytes 262160 | tf_op jit(solution)/shard_map/reduce_scatter | solution.py:109
  (255 shorter events, 118.6 us)
Async XLA Ops:
  7.2 3.8 copy-start
  7.2 93.0 %all-gather.5.cloned.1.call-start = ((), (), s32[]{:S(2)}) async-start(), calls=%async_computation.2 | async-start | bytes 2228224 | tf_op jit(solution)/shard_map/all_gather | solution.py:64
  7.9 200.6 %all-gather.3.cloned.1.call-start = ((), (), s32[]{:S(2)}) async-start(), calls=%async_computation.1 | async-start | bytes 4325376 | tf_op jit(solution)/shard_map/all_gather | solution.py:58
  8.7 506.9 %reduce-scatter.2.cloned.1.call-start = ((), (), s32[]{:S(2)}) async-start(), calls=%async_computation.3 | async-start | bytes 4456448 | tf_op jit(solution)/shard_map/reduce_scatter | solution.py:109
  10.9 203.2 %copy-start.1 = (f32[256,512]{1,0:T(8,128)}, f32[256,512]{1,0:T(8,128)S(1)}, u32[]{:S(2)}) copy-start(f32[256,512]{1,0:T(8,128)S(1)} %get-tuple-element.301) | copy-start | bytes 1572868
  10.9 203.2 %copy-start.3 = (f32[256,512]{1,0:T(8,128)}, f32[256,512]{1,0:T(8,128)S(1)}, u32[]{:S(2)}) copy-start(f32[256,512]{1,0:T(8,128)S(1)} %get-tuple-element.302) | copy-start | bytes 1572868
  11.4 197.1 %copy-start.8 = (bf16[256,256]{1,0:T(8,128)(2,1)S(1)}, bf16[256,256]{1,0:T(8,128)(2,1)}, u32[]{:S(2)}) copy-start(bf16[256,256]{1,0:T(8,128)(2,1)} %param.8) | copy-start | bytes 393220
  100.2 3.3 copy-start.6
  208.5 5.2 copy-start.7
  219.2 7.5 %collective-permute-start = (bf16[256,256]{1,0:T(8,128)(2,1)S(1)}, bf16[256,256]{1,0:T(8,128)(2,1)S(1)}, u32[]{:S(2)}, u32[]{:S(2)}) collective-permute-start(bf16[256,256]{1,0:T(8,128)(2,1)S(1)} %get-tuple-element.374), channel_id=1, source_target_pairs={{32,0},{64,32},{96,64},{128,96},{160,128},{192,160},{224,192},{256... | collective-permute-start | bytes 393224 | tf_op jit(solution)/shard_map/while/body/eval_jaxpr/ppermute | solution.py:12
  231.0 6.9 %collective-permute-start = (bf16[256,256]{1,0:T(8,128)(2,1)S(1)}, bf16[256,256]{1,0:T(8,128)(2,1)S(1)}, u32[]{:S(2)}, u32[]{:S(2)}) collective-permute-start(bf16[256,256]{1,0:T(8,128)(2,1)S(1)} %get-tuple-element.374), channel_id=1, source_target_pairs={{32,0},{64,32},{96,64},{128,96},{160,128},{192,160},{224,192},{256... | collective-permute-start | bytes 393224 | tf_op jit(solution)/shard_map/while/body/eval_jaxpr/ppermute | solution.py:12
  242.1 6.9 %collective-permute-start = (bf16[256,256]{1,0:T(8,128)(2,1)S(1)}, bf16[256,256]{1,0:T(8,128)(2,1)S(1)}, u32[]{:S(2)}, u32[]{:S(2)}) collective-permute-start(bf16[256,256]{1,0:T(8,128)(2,1)S(1)} %get-tuple-element.374), channel_id=1, source_target_pairs={{32,0},{64,32},{96,64},{128,96},{160,128},{192,160},{224,192},{256... | collective-permute-start | bytes 393224 | tf_op jit(solution)/shard_map/while/body/eval_jaxpr/ppermute | solution.py:12
  253.2 7.4 %collective-permute-start = (bf16[256,256]{1,0:T(8,128)(2,1)S(1)}, bf16[256,256]{1,0:T(8,128)(2,1)S(1)}, u32[]{:S(2)}, u32[]{:S(2)}) collective-permute-start(bf16[256,256]{1,0:T(8,128)(2,1)S(1)} %get-tuple-element.374), channel_id=1, source_target_pairs={{32,0},{64,32},{96,64},{128,96},{160,128},{192,160},{224,192},{256... | collective-permute-start | bytes 393224 | tf_op jit(solution)/shard_map/while/body/eval_jaxpr/ppermute | solution.py:12
  264.9 8.8 %collective-permute-start = (bf16[256,256]{1,0:T(8,128)(2,1)S(1)}, bf16[256,256]{1,0:T(8,128)(2,1)S(1)}, u32[]{:S(2)}, u32[]{:S(2)}) collective-permute-start(bf16[256,256]{1,0:T(8,128)(2,1)S(1)} %get-tuple-element.374), channel_id=1, source_target_pairs={{32,0},{64,32},{96,64},{128,96},{160,128},{192,160},{224,192},{256... | collective-permute-start | bytes 393224 | tf_op jit(solution)/shard_map/while/body/eval_jaxpr/ppermute | solution.py:12
  278.0 9.0 %collective-permute-start = (bf16[256,256]{1,0:T(8,128)(2,1)S(1)}, bf16[256,256]{1,0:T(8,128)(2,1)S(1)}, u32[]{:S(2)}, u32[]{:S(2)}) collective-permute-start(bf16[256,256]{1,0:T(8,128)(2,1)S(1)} %get-tuple-element.374), channel_id=1, source_target_pairs={{32,0},{64,32},{96,64},{128,96},{160,128},{192,160},{224,192},{256... | collective-permute-start | bytes 393224 | tf_op jit(solution)/shard_map/while/body/eval_jaxpr/ppermute | solution.py:12
  291.2 9.0 %collective-permute-start = (bf16[256,256]{1,0:T(8,128)(2,1)S(1)}, bf16[256,256]{1,0:T(8,128)(2,1)S(1)}, u32[]{:S(2)}, u32[]{:S(2)}) collective-permute-start(bf16[256,256]{1,0:T(8,128)(2,1)S(1)} %get-tuple-element.374), channel_id=1, source_target_pairs={{32,0},{64,32},{96,64},{128,96},{160,128},{192,160},{224,192},{256... | collective-permute-start | bytes 393224 | tf_op jit(solution)/shard_map/while/body/eval_jaxpr/ppermute | solution.py:12
  304.5 9.0 %collective-permute-start = (bf16[256,256]{1,0:T(8,128)(2,1)S(1)}, bf16[256,256]{1,0:T(8,128)(2,1)S(1)}, u32[]{:S(2)}, u32[]{:S(2)}) collective-permute-start(bf16[256,256]{1,0:T(8,128)(2,1)S(1)} %get-tuple-element.374), channel_id=1, source_target_pairs={{32,0},{64,32},{96,64},{128,96},{160,128},{192,160},{224,192},{256... | collective-permute-start | bytes 393224 | tf_op jit(solution)/shard_map/while/body/eval_jaxpr/ppermute | solution.py:12
  317.8 9.0 %collective-permute-start = (bf16[256,256]{1,0:T(8,128)(2,1)S(1)}, bf16[256,256]{1,0:T(8,128)(2,1)S(1)}, u32[]{:S(2)}, u32[]{:S(2)}) collective-permute-start(bf16[256,256]{1,0:T(8,128)(2,1)S(1)} %get-tuple-element.374), channel_id=1, source_target_pairs={{32,0},{64,32},{96,64},{128,96},{160,128},{192,160},{224,192},{256... | collective-permute-start | bytes 393224 | tf_op jit(solution)/shard_map/while/body/eval_jaxpr/ppermute | solution.py:12
  331.0 9.0 %collective-permute-start = (bf16[256,256]{1,0:T(8,128)(2,1)S(1)}, bf16[256,256]{1,0:T(8,128)(2,1)S(1)}, u32[]{:S(2)}, u32[]{:S(2)}) collective-permute-start(bf16[256,256]{1,0:T(8,128)(2,1)S(1)} %get-tuple-element.374), channel_id=1, source_target_pairs={{32,0},{64,32},{96,64},{128,96},{160,128},{192,160},{224,192},{256... | collective-permute-start | bytes 393224 | tf_op jit(solution)/shard_map/while/body/eval_jaxpr/ppermute | solution.py:12
  344.2 9.3 %collective-permute-start = (bf16[256,256]{1,0:T(8,128)(2,1)S(1)}, bf16[256,256]{1,0:T(8,128)(2,1)S(1)}, u32[]{:S(2)}, u32[]{:S(2)}) collective-permute-start(bf16[256,256]{1,0:T(8,128)(2,1)S(1)} %get-tuple-element.374), channel_id=1, source_target_pairs={{32,0},{64,32},{96,64},{128,96},{160,128},{192,160},{224,192},{256... | collective-permute-start | bytes 393224 | tf_op jit(solution)/shard_map/while/body/eval_jaxpr/ppermute | solution.py:12
  357.8 10.6 %collective-permute-start = (bf16[256,256]{1,0:T(8,128)(2,1)S(1)}, bf16[256,256]{1,0:T(8,128)(2,1)S(1)}, u32[]{:S(2)}, u32[]{:S(2)}) collective-permute-start(bf16[256,256]{1,0:T(8,128)(2,1)S(1)} %get-tuple-element.374), channel_id=1, source_target_pairs={{32,0},{64,32},{96,64},{128,96},{160,128},{192,160},{224,192},{256... | collective-permute-start | bytes 393224 | tf_op jit(solution)/shard_map/while/body/eval_jaxpr/ppermute | solution.py:12
  372.7 9.5 %collective-permute-start = (bf16[256,256]{1,0:T(8,128)(2,1)S(1)}, bf16[256,256]{1,0:T(8,128)(2,1)S(1)}, u32[]{:S(2)}, u32[]{:S(2)}) collective-permute-start(bf16[256,256]{1,0:T(8,128)(2,1)S(1)} %get-tuple-element.374), channel_id=1, source_target_pairs={{32,0},{64,32},{96,64},{128,96},{160,128},{192,160},{224,192},{256... | collective-permute-start | bytes 393224 | tf_op jit(solution)/shard_map/while/body/eval_jaxpr/ppermute | solution.py:12
  386.4 8.8 %collective-permute-start = (bf16[256,256]{1,0:T(8,128)(2,1)S(1)}, bf16[256,256]{1,0:T(8,128)(2,1)S(1)}, u32[]{:S(2)}, u32[]{:S(2)}) collective-permute-start(bf16[256,256]{1,0:T(8,128)(2,1)S(1)} %get-tuple-element.374), channel_id=1, source_target_pairs={{32,0},{64,32},{96,64},{128,96},{160,128},{192,160},{224,192},{256... | collective-permute-start | bytes 393224 | tf_op jit(solution)/shard_map/while/body/eval_jaxpr/ppermute | solution.py:12
  399.5 8.4 %collective-permute-start = (bf16[256,256]{1,0:T(8,128)(2,1)S(1)}, bf16[256,256]{1,0:T(8,128)(2,1)S(1)}, u32[]{:S(2)}, u32[]{:S(2)}) collective-permute-start(bf16[256,256]{1,0:T(8,128)(2,1)S(1)} %get-tuple-element.374), channel_id=1, source_target_pairs={{32,0},{64,32},{96,64},{128,96},{160,128},{192,160},{224,192},{256... | collective-permute-start | bytes 393224 | tf_op jit(solution)/shard_map/while/body/eval_jaxpr/ppermute | solution.py:12
  416.6 1.0 copy-start.2
  416.6 1.2 copy-start.4
  416.6 1.4 copy-start.5
Sparse Core Ops, SparseCore 0:
  10.1 90.0 all-gather.4
  103.3 105.1 all-gather.2
  416.8 98.7 reduce-scatter.1
where the time goes:
time: 525 us; the launch traced here: 522 us
  waiting for transfers between devices  355 us (68%)
  matrix products  55.7 us (11%)
  other arithmetic  47 us (9%)
  local copies, waits for them, and re-layouts  29.2 us (6%)
  starting transfers between devices  19.5 us (4%)
  between operations  13.9 us (3%)
    all_gather x1, waiting for transfers between devices, shards(): lax.all_gather(out_grad, 'ch', axis=1, tiled=True)  104 us
    reduce_scatter x1, waiting for transfers between devices, shards(): lax.psum_scatter(scaled, 'ctx', scatter_dimension=0, tiled=True)  95.8 us
    all_gather x1, waiting for transfers between devices, shards(): taps = lax.all_gather(filter_taps, 'ctx', axis=0, tiled=True)  88.8 us
    ppermute x15, waiting for transfers between devices, shifted(): lax.ppermute(value, axis, [(source, source + steps) for source in range(l...  65.4 us
    add x15, other arithmetic, visit(): total = total + correlate(slab_spec, filter_spectrum(lag_index))  32.1 us
    dot_general x33, matrix products, spectrum(): jnp.dot(table[:, :values.shape[0]], values.astype(jnp.float32), precision...  31.5 us
    ppermute x15, starting transfers between devices, shifted(): lax.ppermute(value, axis, [(source, source + steps) for source in range(l...  19.4 us
    dynamic_slice x30, local copies, waits for them, and re-layouts, visit(): current = lax.dynamic_slice_in_dim(lag_totals, start, period, 0)  19.2 us
  transfers between devices with their start and end apart: 18, of which 18 were waited for; matrix products, arithmetic and copies ran while one was open for 10% of the time, Pallas kernels for 0%

commit v1 on v0

v1 whole, which is shorter than its diff:
```python
import functools
import math

import jax
import jax.numpy as jnp
import numpy as np
from jax import lax
from jax.experimental import pallas as pl
from jax.experimental.pallas import tpu as pltpu
from jax.sharding import PartitionSpec as P

BF = jnp.bfloat16
F32 = jnp.float32
VMEM_LIMIT = 48 * 1024 * 1024


def halves(table):
    high = table.astype(jnp.bfloat16)
    return high, (table - high.astype(np.float64)).astype(jnp.bfloat16)


def tables(block):
    angle = np.pi * (2 * np.arange(block) + 1)[None, :] / (2 * block)
    sample = np.arange(2 * block)[:, None]
    forward = np.concatenate([np.cos(sample * angle), np.sin(sample * angle)], axis=1)
    lag = block - np.arange(block)[None, :]
    inverse = np.concatenate([np.cos(lag * angle.T), np.sin(lag * angle.T)], axis=0) / block
    return halves(forward) + halves(inverse)


def dot(a, b):
    return jnp.dot(a, b, preferred_element_type=F32)


def window_kernel(moved_ref, high_ref, low_ref, out_ref):
    blocks, _, lanes, block = moved_ref.shape
    rows = blocks * lanes
    for which in range(2):
        now = moved_ref[:, which].reshape(rows, block)
        before = jnp.concatenate([jnp.zeros((lanes, block), BF), now[: rows - lanes]], axis=0)
        window = jnp.concatenate([before, now], axis=1)
        spectrum = dot(window, high_ref[...]) + dot(window, low_ref[...])
        out_ref[which] = spectrum.reshape(blocks, lanes, 2 * block)


def project_kernel(side_ref, weight_ref, grad_ref, gate_ref, out_ref, total):
    step = pl.program_id(0)
    size = gate_ref.shape[0]

    @pl.when(step == 0)
    def _():
        total[...] = jnp.zeros_like(total)

    side = side_ref[0]
    acc = total[...]
    for core in range(2):
        for far in range(2):
            at = (jnp.where(far == 0, side, 1 - side) * 2 + core) * size
            weight = weight_ref[:, pl.ds(pl.multiple_of(at, size), size)]
            acc += lax.dot_general(
                weight, grad_ref[core, far], (((1,), (1,)), ((), ())), preferred_element_type=F32
            )
    total[...] = acc

    @pl.when(step == pl.num_programs(0) - 1)
    def _():
        out_ref[...] = (gate_ref[...].astype(F32).T * total[...]).astype(BF)


def correlate_kernel(scale, grad_ref, window_ref, high_ref, low_ref, ihigh_ref, ilow_ref, out_ref, spec, cross):
    blocks, lanes, block = grad_ref.shape
    rows = blocks * lanes
    grad = grad_ref[...].reshape(rows, block)
    spec[...] = (dot(grad, high_ref[...]) + dot(grad, low_ref[...])).reshape(blocks, lanes, 2 * block)
    zero = jnp.zeros((lanes, block), F32)
    for first in range(blocks):

        def add(d, totals, first=first):
            re, im = spec[first + d, :, :block], spec[first + d, :, block:]
            out = []
            for which in range(2):
                wre, wim = window_ref[which, d, :, :block], window_ref[which, d, :, block:]
                out.append(totals[2 * which] + (re * wre + im * wim))
                out.append(totals[2 * which + 1] + (re * wim - im * wre))
            return tuple(out)

        totals = (zero,) * 4
        for d in range(blocks - first):
            totals = add(d, totals)
        for which in range(2):
            cross[which, first, :, :block] = totals[2 * which]
            cross[which, first, :, block:] = totals[2 * which + 1]
    for which in range(2):
        full = cross[which].reshape(rows, 2 * block)
        high = full.astype(BF)
        low = (full - high.astype(F32)).astype(BF)
        lags = dot(high, ihigh_ref[...]) + dot(high, ilow_ref[...]) + dot(low, ihigh_ref[...])
        if which == 1:
            lags = lags * scale
        out_ref[:, which] = lags.astype(BF).reshape(blocks, lanes, block)


def finish_kernel(moved_ref, first_ref, second_ref):
    groups, _, lanes, block = moved_ref.shape
    for which, out_ref in enumerate((first_ref, second_ref)):
        out_ref[...] = moved_ref[:, which].reshape(groups * lanes, block).astype(F32).T


def whole(n):
    return [pl.BlockSpec(memory_space=pltpu.VMEM)] * n


def params():
    return pltpu.CompilerParams(vmem_limit_bytes=VMEM_LIMIT)


def shards(conv_input, gate, out_grad, out_weight, filter_taps):
    block, channels = conv_input.shape
    blocks = lax.axis_size("ctx")
    lanes = channels // blocks
    members = lax.axis_size("ch")
    rounds = members // 4
    fhigh, flow, ihigh, ilow = tables(block)

    other = lax.ppermute(out_grad, "ch", [(i, i ^ 2) for i in range(members)])
    near = [[4 * z + 2 * y + c for z in range(rounds) for c in range(2)] for y in range(2)]
    gathered = lax.all_gather(jnp.stack([out_grad, other]), "ch", axis=0, tiled=False, axis_index_groups=near)

    def columns(value):
        return value.T.reshape(blocks, lanes, block)

    sequences = jnp.stack([columns(filter_taps), columns(conv_input)], axis=1)
    sequences = lax.all_to_all(sequences, "ctx", split_axis=0, concat_axis=0, tiled=True)
    windows = pl.pallas_call(
        window_kernel,
        out_shape=jax.ShapeDtypeStruct((2, blocks, lanes, 2 * block), F32),
        in_specs=whole(3),
        out_specs=whole(1)[0],
        compiler_params=params(),
    )(sequences, fhigh, flow)

    side = (lax.axis_index("ch") // 2 % 2).astype(jnp.int32).reshape(1)
    gated = pl.pallas_call(
        project_kernel,
        grid=(rounds,),
        out_shape=jax.ShapeDtypeStruct((channels, block), BF),
        in_specs=[
            pl.BlockSpec(memory_space=pltpu.SMEM),
            pl.BlockSpec((channels, 4 * channels), lambda z: (0, z)),
            pl.BlockSpec((2, 2, block, channels), lambda z: (z, 0, 0, 0)),
            pl.BlockSpec((block, channels), lambda z: (0, 0)),
        ],
        out_specs=pl.BlockSpec((channels, block), lambda z: (0, 0)),
        scratch_shapes=[pltpu.VMEM((channels, block), F32)],
        compiler_params=params(),
    )(side, out_weight, gathered, gate)

    moved = lax.all_to_all(gated.reshape(blocks, lanes, block), "ctx", split_axis=0, concat_axis=0, tiled=True)
    lags = pl.pallas_call(
        functools.partial(correlate_kernel, 1.0 / math.sqrt(blocks * block)),
        out_shape=jax.ShapeDtypeStruct((blocks, 2, lanes, block), BF),
        in_specs=whole(6),
        out_specs=whole(1)[0],
        scratch_shapes=[
            pltpu.VMEM((blocks, lanes, 2 * block), F32),
            pltpu.VMEM((2, blocks, lanes, 2 * block), F32),
        ],
        compiler_params=params(),
    )(moved, windows, fhigh[:block], flow[:block], ihigh, ilow)
    lags = lax.all_to_all(lags, "ctx", split_axis=0, concat_axis=0, tiled=True)
    return pl.pallas_call(
        finish_kernel,
        out_shape=[jax.ShapeDtypeStruct((block, channels), F32)] * 2,
        in_specs=whole(1),
        out_specs=whole(2),
        compiler_params=params(),
    )(lags)


def solution(mesh):
    return jax.shard_map(
        shards,
        mesh=mesh,
        in_specs=(P("ctx", "ch"), P("ctx", "ch"), P("ctx", "ch"), P("ch", None), P("ctx", "ch")),
        out_specs=(P("ctx", "ch"), P("ctx", "ch")),
        check_vma=False,
    )
```

time: 525 us -> 123 us (0.23)
  the two profiles are of different devices: /device:TPU:64 before, /device:TPU:1 now
where the time goes in v1:
time: 123 us; the launch traced here: 122 us
  waiting for transfers between devices  54.2 us (44%)
  starting transfers between devices  22.9 us (19%)
  between operations  14.2 us (12%)
  blocking collectives  12.6 us (10%)
  Pallas kernels  10.8 us (9%)
  local copies, waits for them, and re-layouts  5.13 us (4%)
  other arithmetic  2.36 us (2%)
    all_gather x1, waiting for transfers between devices, shards(): lax.all_gather(jnp.stack([out_grad, other]), 'ch', axis=0, tiled=False, a...  41.8 us
    all_to_all x1, blocking collectives, shards(): lags = lax.all_to_all(lags, 'ctx', split_axis=0, concat_axis=0, tiled=True)  12.6 us
    ppermute x1, starting transfers between devices, shards(): other = lax.ppermute(out_grad, 'ch', [(i, i ^ 2) for i in range(members)])  8.28 us
    all_to_all x1, starting transfers between devices, shards(): lax.all_to_all(sequences, 'ctx', split_axis=0, concat_axis=0, tiled=True)  7.7 us
    all_to_all x1, waiting for transfers between devices, shards(): lax.all_to_all(gated.reshape(blocks, lanes, block), 'ctx', split_axis=0,...  7.15 us
    pallas_call x1, Pallas kernels, shards(): pl.pallas_call(project_kernel, grid=(rounds,), out_shape=jax.ShapeDtypeSt...  7.14 us
    all_to_all x1, starting transfers between devices, shards(): lax.all_to_all(gated.reshape(blocks, lanes, block), 'ctx', split_axis=0,...  6.84 us
    ppermute x1, waiting for transfers between devices, shards(): other = lax.ppermute(out_grad, 'ch', [(i, i ^ 2) for i in range(members)])  5.18 us
  transfers between devices with their start and end apart: 4, of which 3 were waited for; matrix products, arithmetic and copies ran while one was open for 2% of the time, Pallas kernels for 6%

profile of v1, /device:TPU:1, one launch (start us, length us, event | category | flops | bytes accessed | tf_op | source)
XLA Modules:
  0.0 122.1 jit_solution(4187746976283005316)
XLA Ops:
  7.2 0.0 all-gather.3.cloned.1.call-start
  7.2 8.3 %collective-permute-start = (bf16[256,256]{1,0:T(8,128)(2,1)}, bf16[256,256]{1,0:T(8,128)(2,1)S(1)}, u32[]{:S(2)}, u32[]{:S(2)}) collective-permute-start(bf16[256,256]{1,0:T(8,128)(2,1)} %param.13), channel_id=1, source_target_pairs={{0,2},{1,3},{2,0},{3,1},{4,6},{5,7},{6,4},{7,5},{8,10},{9,11},{10,... | collective-permute-start | bytes 393224 | tf_op jit(solution)/shard_map/ppermute | solution.py:125
  15.5 5.2 %collective-permute-done = bf16[256,256]{1,0:T(8,128)(2,1)S(1)} collective-permute-done((bf16[256,256]{1,0:T(8,128)(2,1)}, bf16[256,256]{1,0:T(8,128)(2,1)S(1)}, u32[]{:S(2)}, u32[]{:S(2)}) %collective-permute-start) | collective-permute-done | bytes 131104 | tf_op jit(solution)/shard_map/ppermute | solution.py:125
  20.7 1.6 %pad_maximum_fusion = bf16[2,256,256]{2,1,0:T(8,128)(2,1)} fusion(bf16[1,256,256]{2,1,0:T(8,128)(2,1)S(1)} %bitcast.15, bf16[1,256,256]{2,1,0:T(8,128)(2,1)} %bitcast.14), kind=kLoop, calls=%fused_computation | loop fusion | flops 131072 | bytes 524288 | tf_op jit(solution)/shard_map/stack | solution.py:127
  22.3 0.0 all-gather.3.cloned.1.call-update
  22.3 1.0 copy.15
  23.3 1.0 copy.16
  24.4 0.7 pad_maximum_fusion.1
  25.1 7.7 %all-to-all-start.1 = ((bf16[16,2,16,256]{3,2,1,0:T(8,128)(2,1)}), bf16[16,2,16,256]{3,2,1,0:T(8,128)(2,1)S(1)}, u32[]{:S(2)}, u32[]{:S(2)}) async-start(bf16[16,2,16,256]{3,2,1,0:T(8,128)(2,1)} %pad_maximum_fusion.1), calls=%async_computation.1 | async-start | bytes 524288 | tf_op jit(solution)/shard_map/all_to_all | solution.py:133
  32.8 41.8 %all-gather.3.cloned.1.call-done = bf16[32,256,256]{2,1,0:T(8,128)(2,1)} async-done(((bf16[2,256,256]{2,1,0:T(8,128)(2,1)}), bf16[32,256,256]{2,1,0:T(8,128)(2,1)}) %all-gather.3.cloned.1.call-update) | async-done | bytes 4194320 | tf_op jit(solution)/shard_map/all_gather | solution.py:127
  74.6 0.0 copy-start
  74.6 2.2 %copy-done = bf16[256,8192]{1,0:T(8,128)(2,1)S(1)} copy-done((bf16[256,8192]{1,0:T(8,128)(2,1)S(1)}, bf16[256,8192]{1,0:T(8,128)(2,1)}, u32[]{:S(2)}) %copy-start) | copy-done | bytes 4194328
  76.8 0.0 copy-start.7
  76.8 0.9 copy-done.7
  77.7 0.0 copy-start.1
  77.7 0.0 copy-start.2
  77.7 0.0 copy-start.5
  77.8 0.0 copy-start.6
  77.8 7.1 %shard_map.122 = bf16[256,256]{1,0:T(8,128)(2,1)} custom-call(s32[1]{0:T(128)} %bitcast.side_ref, bf16[256,8192]{1,0:T(8,128)(2,1)S(1)} %copy-done, bf16[16,2,256,256]{3,2,1,0:T(8,128)(2,1)} %bitcast.9, bf16[256,256]{1,0:T(8,128)(2,1)S(1)} %copy-done.7), custom_call_target="tpu_custom_call" | custom-call | tf_op jit(solution)/shard_map/pallas_call | solution.py:143
  84.9 0.0 all-to-all-done.1.moved_ref
  84.9 6.8 %all-to-all-start = ((bf16[16,16,256]{2,1,0:T(8,128)(2,1)}), bf16[16,16,256]{2,1,0:T(8,128)(2,1)S(1)}, u32[]{:S(2)}, u32[]{:S(2)}) async-start(bf16[16,16,256]{2,1,0:T(8,128)(2,1)} %bitcast.4), calls=%async_computation | async-start | bytes 262144 | tf_op jit(solution)/shard_map/all_to_all | solution.py:158
  91.8 0.0 copy-done.1
  91.8 0.0 copy-done.2
  91.8 0.7 shard_map.123.window_ref
  92.5 7.2 %all-to-all-done.grad_ref = bf16[16,16,256]{2,1,0:T(8,128)(2,1)S(1)} async-done(((bf16[16,16,256]{2,1,0:T(8,128)(2,1)}), bf16[16,16,256]{2,1,0:T(8,128)(2,1)S(1)}, u32[]{:S(2)}, u32[]{:S(2)}) %all-to-all-start) | async-done | bytes 131104 | tf_op jit(solution)/shard_map/all_to_all | solution.py:158
  99.6 0.0 copy-done.3
  99.6 0.0 copy-done.4
  99.7 0.0 copy-done.5
  99.7 0.0 copy-done.6
  99.7 2.1 %shard_map.124 = bf16[16,2,16,256]{3,2,1,0:T(8,128)(2,1)S(1)} custom-call(bf16[16,16,256]{2,1,0:T(8,128)(2,1)S(1)} %all-to-all-done.grad_ref, f32[2,16,16,512]{3,2,1,0:T(8,128)S(1)} %shard_map.123.window_ref, bf16[256,512]{1,0:T(8,128)(2,1)S(1)} %copy-done.3, bf16[256,512]{1,0:T(8,128)(2,1)S(1)} %copy-done.4, bf16[512,256]{1,0:T(8,128)(2,1)S(1)} %copy-done.5, ...), custom_call_target="tpu_custom_call" | custom-call | tf_op jit(solution)/shard_map/pallas_call | solution.py:159
  101.8 12.6 %all_to_all.15.moved_ref = bf16[16,2,16,256]{3,2,1,0:T(8,128)(2,1)S(1)} all-to-all(bf16[16,2,16,256]{3,2,1,0:T(8,128)(2,1)S(1)} %shard_map.124), channel_id=1, replica_groups=mesh['ctx'=16,'ch'=32] {'ctx'}, dimensions={0} | all-to-all | bytes 524288 | tf_op jit(solution)/shard_map/all_to_all | solution.py:170
  114.4 0.9 shard_map.125
  (2 shorter events, 0.0 us)
Async XLA Ops:
  7.2 67.5 %all-gather.3.cloned.1.call-start = ((), (), s32[]{:S(2)}) async-start(), calls=%async_computation.3 | async-start | bytes 4456448 | tf_op jit(solution)/shard_map/all_gather | solution.py:127
  7.2 13.5 %collective-permute-start = (bf16[256,256]{1,0:T(8,128)(2,1)}, bf16[256,256]{1,0:T(8,128)(2,1)S(1)}, u32[]{:S(2)}, u32[]{:S(2)}) collective-permute-start(bf16[256,256]{1,0:T(8,128)(2,1)} %param.13), channel_id=1, source_target_pairs={{0,2},{1,3},{2,0},{3,1},{4,6},{5,7},{6,4},{7,5},{8,10},{9,11},{10,... | collective-permute-start | bytes 393224 | tf_op jit(solution)/shard_map/ppermute | solution.py:125
  25.1 59.8 %all-to-all-start.1 = ((bf16[16,2,16,256]{3,2,1,0:T(8,128)(2,1)}), bf16[16,2,16,256]{3,2,1,0:T(8,128)(2,1)S(1)}, u32[]{:S(2)}, u32[]{:S(2)}) async-start(bf16[16,2,16,256]{3,2,1,0:T(8,128)(2,1)} %pad_maximum_fusion.1), calls=%async_computation.1 | async-start | bytes 524288 | tf_op jit(solution)/shard_map/all_to_all | solution.py:133
  74.6 2.2 %copy-start = (bf16[256,8192]{1,0:T(8,128)(2,1)S(1)}, bf16[256,8192]{1,0:T(8,128)(2,1)}, u32[]{:S(2)}) copy-start(bf16[256,8192]{1,0:T(8,128)(2,1)} %weight_ref.1) | copy-start | bytes 12582916
  76.8 0.9 copy-start.7
  77.7 14.0 %copy-start.1 = (bf16[512,512]{1,0:T(8,128)(2,1)S(1)}, bf16[512,512]{1,0:T(8,128)(2,1)}, u32[]{:S(2)}) copy-start(bf16[512,512]{1,0:T(8,128)(2,1)} %constant.40.clone.high_ref) | copy-start | bytes 1572868
  77.7 14.0 %copy-start.2 = (bf16[512,512]{1,0:T(8,128)(2,1)S(1)}, bf16[512,512]{1,0:T(8,128)(2,1)}, u32[]{:S(2)}) copy-start(bf16[512,512]{1,0:T(8,128)(2,1)} %constant.41.clone.low_ref) | copy-start | bytes 1572868
  77.7 21.9 %copy-start.3 = (bf16[256,512]{1,0:T(8,128)(2,1)S(1)}, bf16[256,512]{1,0:T(8,128)(2,1)}, u32[]{:S(2)}) copy-start(bf16[256,512]{1,0:T(8,128)(2,1)} %constant.42.clone.high_ref) | copy-start | bytes 786436
  77.7 21.9 %copy-start.4 = (bf16[256,512]{1,0:T(8,128)(2,1)S(1)}, bf16[256,512]{1,0:T(8,128)(2,1)}, u32[]{:S(2)}) copy-start(bf16[256,512]{1,0:T(8,128)(2,1)} %constant.43.clone.low_ref) | copy-start | bytes 786436
  77.7 21.9 %copy-start.5 = (bf16[512,256]{1,0:T(8,128)(2,1)S(1)}, bf16[512,256]{1,0:T(8,128)(2,1)}, u32[]{:S(2)}) copy-start(bf16[512,256]{1,0:T(8,128)(2,1)} %constant.44.clone.ihigh_ref) | copy-start | bytes 786436
  77.8 21.9 %copy-start.6 = (bf16[512,256]{1,0:T(8,128)(2,1)S(1)}, bf16[512,256]{1,0:T(8,128)(2,1)}, u32[]{:S(2)}) copy-start(bf16[512,256]{1,0:T(8,128)(2,1)} %constant.45.clone.ilow_ref) | copy-start | bytes 786436
  84.9 14.7 %all-to-all-start = ((bf16[16,16,256]{2,1,0:T(8,128)(2,1)}), bf16[16,16,256]{2,1,0:T(8,128)(2,1)S(1)}, u32[]{:S(2)}, u32[]{:S(2)}) async-start(bf16[16,16,256]{2,1,0:T(8,128)(2,1)} %bitcast.4), calls=%async_computation | async-start | bytes 262144 | tf_op jit(solution)/shard_map/all_to_all | solution.py:158
Sparse Core Ops, SparseCore 0:
  22.5 52.1 all-gather.2

commit v2 on v1

--- a/solution.py
+++ b/solution.py
@@ -30,6 +30,65 @@
 
 def dot(a, b):
     return jnp.dot(a, b, preferred_element_type=F32)
+
+
+def slabs(ch, sweeps, size):
+    z, side, core = ch // 4, ch // 2 % 2, ch % 2
+    place = (z + 8 - core) % 8
+    pair, turn = place // 2, 2 * (place % 2) - 1
+    pairs = (pair, pair + turn, pair - turn, pair + 2 * turn)
+    for sweep in sweeps:
+        for far in range(2):
+            towards = side if far == 0 else 1 - side
+            for spot in range(2):
+                at = (2 * (pairs[sweep] + 4) + spot + core) % 8
+                yield sweep, far, spot, pl.multiple_of((at * 4 + towards * 2 + core) * size, size)
+
+
+BOTH_LAST = (((1,), (1,)), ((), ()))
+
+
+def columns_kernel(gate_ref, taps_ref, input_ref, gate_out, send_ref):
+    blocks, _, lanes, block = send_ref.shape
+    gate_out[...] = gate_ref[...].astype(F32).T.astype(BF)
+    for which, ref in enumerate((taps_ref, input_ref)):
+        send_ref[:, which] = ref[...].astype(F32).T.astype(BF).reshape(blocks, lanes, block)
+
+
+def early_kernel(ch_ref, weight_ref, lent_ref, *rest):
+    parts, (sum_ref, kept_ref, slab, slab_done, kept_done) = rest[:6], rest[6:]
+    size = weight_ref.shape[0]
+    first = list(slabs(ch_ref[0], (0, 1, 2), size))
+    last = list(slabs(ch_ref[0], (3,), size))
+    copies, keeps = [], []
+    for which, ref in enumerate((weight_ref, lent_ref)):
+        copies.append([])
+        for n, (_, _, _, at) in enumerate(first):
+            target = slab.at[which, :, pl.ds(n * size, size)]
+            copies[which].append(pltpu.make_async_copy(ref.at[:, pl.ds(at, size)], target, slab_done.at[which, n]))
+        for n, (_, _, _, at) in enumerate(last):
+            target = kept_ref.at[which, :, pl.ds(n * size, size)]
+            keeps.append(pltpu.make_async_copy(ref.at[:, pl.ds(at, size)], target, kept_done.at[which, n]))
+    for copy in copies[0] + copies[1] + keeps:
+        copy.start()
+    grads = jnp.concatenate([parts[2 * sweep + far][spot] for sweep, far, spot, _ in first], axis=1)
+    for which in range(2):
+        for copy in copies[which]:
+            copy.wait()
+        sum_ref[which] = lax.dot_general(slab[which], grads, BOTH_LAST, preferred_element_type=F32)
+    for copy in keeps:
+        copy.wait()
+
+
+def late_kernel(sum_ref, kept_ref, near_ref, far_ref, own_ref, lend_ref):
+    grads = jnp.concatenate([near_ref[0], near_ref[1], far_ref[0], far_ref[1]], axis=1)
+    for which, ref in enumerate((own_ref, lend_ref)):
+        ref[...] = sum_ref[which] + lax.dot_general(kept_ref[which], grads, BOTH_LAST, preferred_element_type=F32)
+
+
+def gate_kernel(ch_ref, own_ref, swapped_ref, gate_ref, out_ref):
+    pre_gate = own_ref[...] + swapped_ref[1 - ch_ref[0] % 2]
+    out_ref[...] = (gate_ref[...].astype(F32) * pre_gate).astype(BF)
 
 
 def window_kernel(moved_ref, high_ref, low_ref, out_ref):
@@ -41,30 +100,6 @@
         window = jnp.concatenate([before, now], axis=1)
         spectrum = dot(window, high_ref[...]) + dot(window, low_ref[...])
         out_ref[which] = spectrum.reshape(blocks, lanes, 2 * block)
-
-
-def project_kernel(side_ref, weight_ref, grad_ref, gate_ref, out_ref, total):
-    step = pl.program_id(0)
-    size = gate_ref.shape[0]
-
-    @pl.when(step == 0)
-    def _():
-        total[...] = jnp.zeros_like(total)
-
-    side = side_ref[0]
-    acc = total[...]
-    for core in range(2):
-        for far in range(2):
-            at = (jnp.where(far == 0, side, 1 - side) * 2 + core) * size
-            weight = weight_ref[:, pl.ds(pl.multiple_of(at, size), size)]
-            acc += lax.dot_general(
-                weight, grad_ref[core, far], (((1,), (1,)), ((), ())), preferred_element_type=F32
-            )
-    total[...] = acc
-
-    @pl.when(step == pl.num_programs(0) - 1)
-    def _():
-        out_ref[...] = (gate_ref[...].astype(F32).T * total[...]).astype(BF)
 
 
 def correlate_kernel(scale, grad_ref, window_ref, high_ref, low_ref, ihigh_ref, ilow_ref, out_ref, spec, cross):
@@ -110,8 +145,8 @@
     return [pl.BlockSpec(memory_space=pltpu.VMEM)] * n
 
 
-def params():
-    return pltpu.CompilerParams(vmem_limit_bytes=VMEM_LIMIT)
+def params(limit=VMEM_LIMIT):
+    return pltpu.CompilerParams(vmem_limit_bytes=limit)
 
 
 def shards(conv_input, gate, out_grad, out_weight, filter_taps):
@@ -119,17 +154,36 @@
     blocks = lax.axis_size("ctx")
     lanes = channels // blocks
     members = lax.axis_size("ch")
-    rounds = members // 4
     fhigh, flow, ihigh, ilow = tables(block)
-
-    other = lax.ppermute(out_grad, "ch", [(i, i ^ 2) for i in range(members)])
-    near = [[4 * z + 2 * y + c for z in range(rounds) for c in range(2)] for y in range(2)]
-    gathered = lax.all_gather(jnp.stack([out_grad, other]), "ch", axis=0, tiled=False, axis_index_groups=near)
-
-    def columns(value):
-        return value.T.reshape(blocks, lanes, block)
-
-    sequences = jnp.stack([columns(filter_taps), columns(conv_input)], axis=1)
+    ch = lax.axis_index("ch").astype(jnp.int32)
+    ch_ref = ch.reshape(1)
+    smem = pl.BlockSpec(memory_space=pltpu.SMEM)
+
+    def spot(z, y, c):
+        return z % 8 * 4 + y * 2 + c
+
+    def neighbours(step):
+        return [
+            [spot(2 * k + (c + step) % 2, y, c), spot(2 * k + 1 + (c + step) % 2, y, c)]
+            for k in range(4) for y in range(2) for c in range(2)
+        ]
+
+    def swap(value, pairs):
+        return lax.ppermute(value, "ch", [(a, b) for pair in pairs for a, b in (pair, pair[::-1])])
+
+    cores = [[i, i + 1] for i in range(0, members, 2)]
+    far = swap(out_grad, [[i, i + 2] for i in range(0, members, 4)] + [[i + 1, i + 3] for i in range(0, members, 4)])
+    near = lax.all_gather(out_grad, "ch", axis=0, tiled=False, axis_index_groups=neighbours(0))
+    columns, sequences = pl.pallas_call(
+        columns_kernel,
+        out_shape=[
+            jax.ShapeDtypeStruct((channels, block), BF),
+            jax.ShapeDtypeStruct((blocks, 2, lanes, block), BF),
+        ],
+        in_specs=whole(3),
+        out_specs=whole(2),
+        compiler_params=params(62 << 20),
+    )(gate, filter_taps, conv_input)
     sequences = lax.all_to_all(sequences, "ctx", split_axis=0, concat_axis=0, tiled=True)
     windows = pl.pallas_call(
         window_kernel,
@@ -138,22 +192,48 @@
         out_specs=whole(1)[0],
         compiler_params=params(),
     )(sequences, fhigh, flow)
-
-    side = (lax.axis_index("ch") // 2 % 2).astype(jnp.int32).reshape(1)
+    lent = swap(out_weight, cores)
+    far, near, lent, columns = lax.optimization_barrier((far, near, lent, columns))
+    far = lax.all_gather(far, "ch", axis=0, tiled=False, axis_index_groups=neighbours(0))
+    near, far = lax.optimization_barrier((near, far))
+    parts = [near, far]
+    for step in (1, 2, 3):
+        near, far = swap(near, neighbours(step)), swap(far, neighbours(step))
+        if step == 2:
+            near, windows = lax.optimization_barrier((near, windows))
+        parts += [near, far]
+
+    early, kept = pl.pallas_call(
+        early_kernel,
+        out_shape=[
+            jax.ShapeDtypeStruct((2, channels, block), F32),
+            jax.ShapeDtypeStruct((2, channels, 4 * channels), BF),
+        ],
+        in_specs=[smem] + [pl.BlockSpec(memory_space=pl.ANY)] * 2 + whole(6),
+        out_specs=whole(2),
+        scratch_shapes=[
+            pltpu.VMEM((2, channels, 12 * channels), BF),
+            pltpu.SemaphoreType.DMA((2, 12)),
+            pltpu.SemaphoreType.DMA((2, 4)),
+        ],
+        compiler_params=params(),
+        cost_estimate=pl.CostEstimate(flops=2 * 2 * 3072 * 256 * 256, bytes_accessed=8 << 20, transcendentals=0),
+    )(ch_ref, out_weight, lent, *parts[:6])
+    own, lend = pl.pallas_call(
+        late_kernel,
+        out_shape=[jax.ShapeDtypeStruct((channels, block), F32)] * 2,
+        in_specs=whole(4),
+        out_specs=whole(2),
+        compiler_params=params(),
+    )(early, kept, *parts[6:])
+    swapped = lax.all_gather(lend, "ch", axis=0, tiled=False, axis_index_groups=cores)
     gated = pl.pallas_call(
-        project_kernel,
-        grid=(rounds,),
+        gate_kernel,
         out_shape=jax.ShapeDtypeStruct((channels, block), BF),
-        in_specs=[
-            pl.BlockSpec(memory_space=pltpu.SMEM),
-            pl.BlockSpec((channels, 4 * channels), lambda z: (0, z)),
-            pl.BlockSpec((2, 2, block, channels), lambda z: (z, 0, 0, 0)),
-            pl.BlockSpec((block, channels), lambda z: (0, 0)),
-        ],
-        out_specs=pl.BlockSpec((channels, block), lambda z: (0, 0)),
-        scratch_shapes=[pltpu.VMEM((channels, block), F32)],
-        compiler_params=params(),
-    )(side, out_weight, gathered, gate)
+        in_specs=[smem] + whole(3),
+        out_specs=whole(1)[0],
+        compiler_params=params(),
+    )(ch_ref, own, swapped, columns)
 
     moved = lax.all_to_all(gated.reshape(blocks, lanes, block), "ctx", split_axis=0, concat_axis=0, tiled=True)
     lags = pl.pallas_call(

time: 123 us -> 101 us (0.82)
  waiting for transfers between devices: 54.2 us -> 3.67 us
  blocking collectives: 12.6 us -> 51.1 us
  between operations: 14.2 us -> 0.84 us
  starting transfers between devices: 22.9 us -> 33 us
  local copies, waits for them, and re-layouts: 5.13 us -> 2.12 us
  other arithmetic: 2.36 us -> 0 us
    all_gather x1 -> x0, waiting for transfers between devices: 41.8 us -> none  [shards(): lax.all_gather(jnp.stack([out_grad, other]), 'ch', axis=0, tiled=False, a...]
    all_gather x0 -> x3, blocking collectives: none -> 27.6 us  [the longest x1 12 us: shards(): lax.all_gather(out_grad, 'ch', axis=0, tiled=False, axis_index_groups=nei...]
    ppermute x1 -> x8, starting transfers between devices: 8.28 us -> 27.9 us  [swap(): lax.ppermute(value, 'ch', [(a, b) for pair in pairs for a, b in (pair, pa...]
    all_to_all x0 -> x1, blocking collectives: none -> 10.7 us  [shards(): lax.all_to_all(gated.reshape(blocks, lanes, block), 'ctx', split_axis=0,...]
    all_to_all x1 -> x0, waiting for transfers between devices: 7.15 us -> none  [shards(): lax.all_to_all(gated.reshape(blocks, lanes, block), 'ctx', split_axis=0,...]
    all_to_all x1 -> x0, starting transfers between devices: 6.84 us -> none  [shards(): lax.all_to_all(gated.reshape(blocks, lanes, block), 'ctx', split_axis=0,...]
    ppermute x1 -> x8, waiting for transfers between devices: 5.18 us -> 1.29 us  [swap(): lax.ppermute(value, 'ch', [(a, b) for pair in pairs for a, b in (pair, pa...]
    all_to_all x1, starting transfers between devices: 7.7 us -> 5.07 us  [shards(): lax.all_to_all(sequences, 'ctx', split_axis=0, concat_axis=0, tiled=True)]
  transfers between devices with their start and end apart: 4 -> 9, of which waited for: 3 -> 2; matrix products, arithmetic and copies ran while one was open for 2% -> 0% of each run, Pallas kernels for 6% -> 6%
where the time goes in v2:
time: 101 us
  blocking collectives  51.1 us (51%)
  starting transfers between devices  33 us (33%)
  Pallas kernels  9.92 us (10%)
  waiting for transfers between devices  3.67 us (4%)
  local copies, waits for them, and re-layouts  2.12 us (2%)
    ppermute x8, starting transfers between devices, swap(): lax.ppermute(value, 'ch', [(a, b) for pair in pairs for a, b in (pair, pa...  27.9 us
    all_to_all x1, blocking collectives, shards(): lags = lax.all_to_all(lags, 'ctx', split_axis=0, concat_axis=0, tiled=True)  12.7 us
    all_gather x1, blocking collectives, shards(): lax.all_gather(out_grad, 'ch', axis=0, tiled=False, axis_index_groups=nei...  12 us
    all_to_all x1, blocking collectives, shards(): lax.all_to_all(gated.reshape(blocks, lanes, block), 'ctx', split_axis=0,...  10.7 us
    all_gather x1, blocking collectives, shards(): lax.all_gather(lend, 'ch', axis=0, tiled=False, axis_index_groups=cores)  9.91 us
    all_gather x1, blocking collectives, shards(): lax.all_gather(far, 'ch', axis=0, tiled=False, axis_index_groups=neighbou...  5.7 us
    all_to_all x1, starting transfers between devices, shards(): lax.all_to_all(sequences, 'ctx', split_axis=0, concat_axis=0, tiled=True)  5.07 us
    pallas_call x1, Pallas kernels, shards(): pl.pallas_call(early_kernel, out_shape=[jax.ShapeDtypeStruct((2, channels...  3.82 us
  transfers between devices with their start and end apart: 9, of which 2 were waited for; matrix products, arithmetic and copies ran while one was open for 0% of the time, Pallas kernels for 6%

profile of v2, /device:TPU:1, one launch (start us, length us, event | category | flops | bytes accessed | tf_op | source)
XLA Modules:
  0.0 100.7 jit_solution(757816270264808278)
XLA Ops:
  0.6 8.8 %collective-permute-start.1 = (bf16[256,8192]{1,0:T(8,128)(2,1)}, bf16[256,8192]{1,0:T(8,128)(2,1)}, u32[]{:S(2)}, u32[]{:S(2)}) collective-permute-start(bf16[256,8192]{1,0:T(8,128)(2,1)} %weight_ref.1), channel_id=1, source_target_pairs={{0,1},{1,0},{2,3},{3,2},{4,5},{5,4},{6,7},{7,6},{8,9},{9,8},{10,11... | collective-permute-start | bytes 12582920 | tf_op jit(solution)/shard_map/ppermute | solution.py:172
  9.4 2.1 %collective-permute-start = (bf16[256,256]{1,0:T(8,128)(2,1)}, bf16[256,256]{1,0:T(8,128)(2,1)S(1)}, u32[]{:S(2)}, u32[]{:S(2)}) collective-permute-start(bf16[256,256]{1,0:T(8,128)(2,1)} %param.13), channel_id=1, source_target_pairs={{0,2},{2,0},{4,6},{6,4},{8,10},{10,8},{12,14},{14,12},{16,18},{18,... | collective-permute-start | bytes 393224 | tf_op jit(solution)/shard_map/ppermute | solution.py:172
  11.5 1.9 %shard_map.122 = (bf16[256,256]{1,0:T(8,128)(2,1)}, bf16[16,2,16,256]{3,2,1,0:T(8,128)(2,1)}) custom-call(bf16[256,256]{1,0:T(8,128)(2,1)} %gate_ref.1, bf16[256,256]{1,0:T(8,128)(2,1)} %taps_ref.1, bf16[256,256]{1,0:T(8,128)(2,1)} %input_ref.1), custom_call_target="tpu_custom_call" | custom-call | tf_op jit(solution)/shard_map/pallas_call | solution.py:177
  13.4 12.0 %all-gather = bf16[512,256]{1,0:T(8,128)(2,1)S(1)} all-gather(bf16[256,256]{1,0:T(8,128)(2,1)} %param.13), channel_id=2, replica_groups={{0,4},{5,9},{2,6},{7,11},{8,12},{13,17},{10,14},{15,19},{16,20},{21,25}..., dimensions={0}, use_global_device_ids=true | all-gather | bytes 393216 | tf_op jit(solution)/shard_map/all_gather | solution.py:176
  25.5 0.0 collective-permute-done
  25.5 5.7 %all-gather.1 = bf16[512,256]{1,0:T(8,128)(2,1)S(1)} all-gather(bf16[256,256]{1,0:T(8,128)(2,1)S(1)} %collective-permute-done), channel_id=3, replica_groups={{0,4},{5,9},{2,6},{7,11},{8,12},{13,17},{10,14},{15,19},{16,20},{21,25}..., dimensions={0}, use_global_device_ids=true | all-gather | bytes 393216 | tf_op jit(solution)/shard_map/all_gather | solution.py:197
  31.2 1.9 %collective-permute-start.2 = (bf16[2,256,256]{2,1,0:T(8,128)(2,1)S(1)}, bf16[2,256,256]{2,1,0:T(8,128)(2,1)S(1)}, u32[]{:S(2)}, u32[]{:S(2)}) collective-permute-start(bf16[2,256,256]{2,1,0:T(8,128)(2,1)S(1)} %bitcast.6), channel_id=1, source_target_pairs={{4,8},{8,4},{1,5},{5,1},{6,10},{10,6},{3,7},{7,3},{12,16},{16,12},... | collective-permute-start | bytes 786440 | tf_op jit(solution)/shard_map/ppermute | solution.py:172
  33.1 3.4 %collective-permute-start.3 = (bf16[2,256,256]{2,1,0:T(8,128)(2,1)S(1)}, bf16[2,256,256]{2,1,0:T(8,128)(2,1)S(1)}, u32[]{:S(2)}, u32[]{:S(2)}) collective-permute-start(bf16[2,256,256]{2,1,0:T(8,128)(2,1)S(1)} %bitcast.8), channel_id=1, source_target_pairs={{4,8},{8,4},{1,5},{5,1},{6,10},{10,6},{3,7},{7,3},{12,16},{16,12},... | collective-permute-start | bytes 786440 | tf_op jit(solution)/shard_map/ppermute | solution.py:172
  36.5 5.1 %all-to-all-start = ((bf16[16,2,16,256]{3,2,1,0:T(8,128)(2,1)}), bf16[16,2,16,256]{3,2,1,0:T(8,128)(2,1)S(1)}, u32[]{:S(2)}, u32[]{:S(2)}) async-start(bf16[16,2,16,256]{3,2,1,0:T(8,128)(2,1)} %get-tuple-element.22), calls=%async_computation | async-start | bytes 524288 | tf_op jit(solution)/shard_map/all_to_all | solution.py:187
  41.5 0.0 collective-permute-done.2.rest_2_
  41.5 4.6 %collective-permute-start.4 = (bf16[2,256,256]{2,1,0:T(8,128)(2,1)S(1)}, bf16[2,256,256]{2,1,0:T(8,128)(2,1)S(1)}, u32[]{:S(2)}, u32[]{:S(2)}) collective-permute-start(bf16[2,256,256]{2,1,0:T(8,128)(2,1)S(1)} %collective-permute-done.2.rest_2_), channel_id=1, source_target_pairs={{0,4},{4,0},{5,9},{9,5},{2,6},{6,2},{7,11},{11,7},{8,12},{12,8},{1... | collective-permute-start | bytes 786440 | tf_op jit(solution)/shard_map/ppermute | solution.py:172
  46.2 1.9 %collective-permute-start.5 = (bf16[2,256,256]{2,1,0:T(8,128)(2,1)S(1)}, bf16[2,256,256]{2,1,0:T(8,128)(2,1)S(1)}, u32[]{:S(2)}, u32[]{:S(2)}) collective-permute-start(bf16[2,256,256]{2,1,0:T(8,128)(2,1)S(1)} %collective-permute-done.3.rest_3_), channel_id=1, source_target_pairs={{0,4},{4,0},{5,9},{9,5},{2,6},{6,2},{7,11},{11,7},{8,12},{12,8},{1... | collective-permute-start | bytes 786440 | tf_op jit(solution)/shard_map/ppermute | solution.py:172
  48.1 2.4 %all-to-all-done.moved_ref = bf16[16,2,16,256]{3,2,1,0:T(8,128)(2,1)S(1)} async-done(((bf16[16,2,16,256]{3,2,1,0:T(8,128)(2,1)}), bf16[16,2,16,256]{3,2,1,0:T(8,128)(2,1)S(1)}, u32[]{:S(2)}, u32[]{:S(2)}) %all-to-all-start) | async-done | bytes 262176 | tf_op jit(solution)/shard_map/all_to_all | solution.py:187
  50.5 1.0 %copy-done = bf16[512,512]{1,0:T(8,128)(2,1)S(1)} copy-done((bf16[512,512]{1,0:T(8,128)(2,1)S(1)}, bf16[512,512]{1,0:T(8,128)(2,1)}, u32[]{:S(2)}) %copy-start) | copy-done | bytes 524312
  51.5 1.0 %copy-done.1 = bf16[512,512]{1,0:T(8,128)(2,1)S(1)} copy-done((bf16[512,512]{1,0:T(8,128)(2,1)S(1)}, bf16[512,512]{1,0:T(8,128)(2,1)}, u32[]{:S(2)}) %copy-start.1) | copy-done | bytes 524312
  52.5 0.7 shard_map.123.window_ref
  53.3 0.0 collective-permute-done.4.rest_4_
  53.3 3.1 %collective-permute-start.6 = (bf16[2,256,256]{2,1,0:T(8,128)(2,1)S(1)}, bf16[2,256,256]{2,1,0:T(8,128)(2,1)S(1)}, u32[]{:S(2)}, u32[]{:S(2)}) collective-permute-start(bf16[2,256,256]{2,1,0:T(8,128)(2,1)S(1)} %collective-permute-done.4.rest_4_), channel_id=1, source_target_pairs={{4,8},{8,4},{1,5},{5,1},{6,10},{10,6},{3,7},{7,3},{12,16},{16,12},... | collective-permute-start | bytes 786440 | tf_op jit(solution)/shard_map/ppermute | solution.py:172
  56.3 2.2 %collective-permute-start.7 = (bf16[2,256,256]{2,1,0:T(8,128)(2,1)S(1)}, bf16[2,256,256]{2,1,0:T(8,128)(2,1)S(1)}, u32[]{:S(2)}, u32[]{:S(2)}) collective-permute-start(bf16[2,256,256]{2,1,0:T(8,128)(2,1)S(1)} %collective-permute-done.5.rest_5_), channel_id=1, source_target_pairs={{4,8},{8,4},{1,5},{5,1},{6,10},{10,6},{3,7},{7,3},{12,16},{16,12},... | collective-permute-start | bytes 786440 | tf_op jit(solution)/shard_map/ppermute | solution.py:172
  58.6 0.0 copy-start.6
  58.6 3.8 %shard_map.124 = (f32[2,256,256]{2,1,0:T(8,128)S(1)}, bf16[2,256,1024]{2,1,0:T(8,128)(2,1)S(1)}) custom-call(s32[1]{0:T(128)} %bitcast.ch_ref, bf16[256,8192]{1,0:T(8,128)(2,1)} %weight_ref.1, bf16[256,8192]{1,0:T(8,128)(2,1)} %collective-permute-done.1.lent_ref, bf16[2,256,256]{2,1,0:T(8,128)(2,1)S(1)} %bitcast.7, bf16[2,256,256]{2,1,0:T(8,128)(2,1)S(1)} %bitcast.9, ...), custom_call_target="tpu_custom_call" | custom-call | flops 805306368 | bytes 8388608 | tf_op jit(solution)/shard_map/pallas_call | solution.py:206
  62.4 0.0 copy-start.2
  62.4 0.0 copy-start.3
  62.4 0.0 copy-start.4
  62.5 0.0 copy-start.5
  62.5 1.3 %collective-permute-done.7.far_ref = bf16[2,256,256]{2,1,0:T(8,128)(2,1)S(1)} collective-permute-done((bf16[2,256,256]{2,1,0:T(8,128)(2,1)S(1)}, bf16[2,256,256]{2,1,0:T(8,128)(2,1)S(1)}, u32[]{:S(2)}, u32[]{:S(2)}) %collective-permute-start.7) | collective-permute-done | bytes 262176 | tf_op jit(solution)/shard_map/ppermute | solution.py:172
  63.8 0.5 shard_map.125
  64.2 9.9 %all-gather.2 = f32[512,256]{1,0:T(8,128)S(1)} all-gather(f32[256,256]{1,0:T(8,128)S(1)} %get-tuple-element.27), channel_id=4, replica_groups={{0,1},{2,3},{4,5},{6,7},{8,9},{10,11},{12,13},{14,15},{16,17},{18,19},{..., dimensions={0}, use_global_device_ids=true | all-gather | bytes 786432 | tf_op jit(solution)/shard_map/all_gather | solution.py:229
  74.2 10.7 %all_to_all.15.grad_ref = bf16[16,16,256]{2,1,0:T(8,128)(2,1)S(1)} all-to-all(bf16[16,16,256]{2,1,0:T(8,128)(2,1)S(1)} %bitcast.10), channel_id=1, replica_groups=mesh['ctx'=16,'ch'=32] {'ctx'}, dimensions={0} | all-to-all | bytes 262144 | tf_op jit(solution)/shard_map/all_to_all | solution.py:238
  84.9 2.1 %shard_map.127 = bf16[16,2,16,256]{3,2,1,0:T(8,128)(2,1)S(1)} custom-call(bf16[16,16,256]{2,1,0:T(8,128)(2,1)S(1)} %all_to_all.15.grad_ref, f32[2,16,16,512]{3,2,1,0:T(8,128)S(1)} %shard_map.123.window_ref, bf16[256,512]{1,0:T(8,128)(2,1)S(1)} %copy-done.2, bf16[256,512]{1,0:T(8,128)(2,1)S(1)} %copy-done.3, bf16[512,256]{1,0:T(8,128)(2,1)S(1)} %copy-done.4, ...), custom_call_target="tpu_custom_call" | custom-call | tf_op jit(solution)/shard_map/pallas_call | solution.py:239
  87.0 12.7 %all_to_all.16.moved_ref = bf16[16,2,16,256]{3,2,1,0:T(8,128)(2,1)S(1)} all-to-all(bf16[16,2,16,256]{3,2,1,0:T(8,128)(2,1)S(1)} %shard_map.127), channel_id=1, replica_groups=mesh['ctx'=16,'ch'=32] {'ctx'}, dimensions={0} | all-to-all | bytes 524288 | tf_op jit(solution)/shard_map/all_to_all | solution.py:250
  99.8 0.9 shard_map.128
  (12 shorter events, 0.1 us)
Async XLA Ops:
  0.6 24.8 %collective-permute-start.1 = (bf16[256,8192]{1,0:T(8,128)(2,1)}, bf16[256,8192]{1,0:T(8,128)(2,1)}, u32[]{:S(2)}, u32[]{:S(2)}) collective-permute-start(bf16[256,8192]{1,0:T(8,128)(2,1)} %weight_ref.1), channel_id=1, source_target_pairs={{0,1},{1,0},{2,3},{3,2},{4,5},{5,4},{6,7},{7,6},{8,9},{9,8},{10,11... | collective-permute-start | bytes 12582920 | tf_op jit(solution)/shard_map/ppermute | solution.py:172
  9.4 16.0 %collective-permute-start = (bf16[256,256]{1,0:T(8,128)(2,1)}, bf16[256,256]{1,0:T(8,128)(2,1)S(1)}, u32[]{:S(2)}, u32[]{:S(2)}) collective-permute-start(bf16[256,256]{1,0:T(8,128)(2,1)} %param.13), channel_id=1, source_target_pairs={{0,2},{2,0},{4,6},{6,4},{8,10},{10,8},{12,14},{14,12},{16,18},{18,... | collective-permute-start | bytes 393224 | tf_op jit(solution)/shard_map/ppermute | solution.py:172
  31.2 10.4 %collective-permute-start.2 = (bf16[2,256,256]{2,1,0:T(8,128)(2,1)S(1)}, bf16[2,256,256]{2,1,0:T(8,128)(2,1)S(1)}, u32[]{:S(2)}, u32[]{:S(2)}) collective-permute-start(bf16[2,256,256]{2,1,0:T(8,128)(2,1)S(1)} %bitcast.6), channel_id=1, source_target_pairs={{4,8},{8,4},{1,5},{5,1},{6,10},{10,6},{3,7},{7,3},{12,16},{16,12},... | collective-permute-start | bytes 786440 | tf_op jit(solution)/shard_map/ppermute | solution.py:172
  33.1 13.1 %collective-permute-start.3 = (bf16[2,256,256]{2,1,0:T(8,128)(2,1)S(1)}, bf16[2,256,256]{2,1,0:T(8,128)(2,1)S(1)}, u32[]{:S(2)}, u32[]{:S(2)}) collective-permute-start(bf16[2,256,256]{2,1,0:T(8,128)(2,1)S(1)} %bitcast.8), channel_id=1, source_target_pairs={{4,8},{8,4},{1,5},{5,1},{6,10},{10,6},{3,7},{7,3},{12,16},{16,12},... | collective-permute-start | bytes 786440 | tf_op jit(solution)/shard_map/ppermute | solution.py:172
  36.5 14.0 %all-to-all-start = ((bf16[16,2,16,256]{3,2,1,0:T(8,128)(2,1)}), bf16[16,2,16,256]{3,2,1,0:T(8,128)(2,1)S(1)}, u32[]{:S(2)}, u32[]{:S(2)}) async-start(bf16[16,2,16,256]{3,2,1,0:T(8,128)(2,1)} %get-tuple-element.22), calls=%async_computation | async-start | bytes 524288 | tf_op jit(solution)/shard_map/all_to_all | solution.py:187
  41.5 11.7 %collective-permute-start.4 = (bf16[2,256,256]{2,1,0:T(8,128)(2,1)S(1)}, bf16[2,256,256]{2,1,0:T(8,128)(2,1)S(1)}, u32[]{:S(2)}, u32[]{:S(2)}) collective-permute-start(bf16[2,256,256]{2,1,0:T(8,128)(2,1)S(1)} %collective-permute-done.2.rest_2_), channel_id=1, source_target_pairs={{0,4},{4,0},{5,9},{9,5},{2,6},{6,2},{7,11},{11,7},{8,12},{12,8},{1... | collective-permute-start | bytes 786440 | tf_op jit(solution)/shard_map/ppermute | solution.py:172
  46.2 10.2 %collective-permute-start.5 = (bf16[2,256,256]{2,1,0:T(8,128)(2,1)S(1)}, bf16[2,256,256]{2,1,0:T(8,128)(2,1)S(1)}, u32[]{:S(2)}, u32[]{:S(2)}) collective-permute-start(bf16[2,256,256]{2,1,0:T(8,128)(2,1)S(1)} %collective-permute-done.3.rest_3_), channel_id=1, source_target_pairs={{0,4},{4,0},{5,9},{9,5},{2,6},{6,2},{7,11},{11,7},{8,12},{12,8},{1... | collective-permute-start | bytes 786440 | tf_op jit(solution)/shard_map/ppermute | solution.py:172
  50.5 1.0 %copy-start = (bf16[512,512]{1,0:T(8,128)(2,1)S(1)}, bf16[512,512]{1,0:T(8,128)(2,1)}, u32[]{:S(2)}) copy-start(bf16[512,512]{1,0:T(8,128)(2,1)} %constant.16.clone.high_ref) | copy-start | bytes 1572868
  51.5 1.0 %copy-start.1 = (bf16[512,512]{1,0:T(8,128)(2,1)S(1)}, bf16[512,512]{1,0:T(8,128)(2,1)}, u32[]{:S(2)}) copy-start(bf16[512,512]{1,0:T(8,128)(2,1)} %constant.17.clone.low_ref) | copy-start | bytes 1572868
  53.3 9.2 %collective-permute-start.6 = (bf16[2,256,256]{2,1,0:T(8,128)(2,1)S(1)}, bf16[2,256,256]{2,1,0:T(8,128)(2,1)S(1)}, u32[]{:S(2)}, u32[]{:S(2)}) collective-permute-start(bf16[2,256,256]{2,1,0:T(8,128)(2,1)S(1)} %collective-permute-done.4.rest_4_), channel_id=1, source_target_pairs={{4,8},{8,4},{1,5},{5,1},{6,10},{10,6},{3,7},{7,3},{12,16},{16,12},... | collective-permute-start | bytes 786440 | tf_op jit(solution)/shard_map/ppermute | solution.py:172
  56.3 7.4 %collective-permute-start.7 = (bf16[2,256,256]{2,1,0:T(8,128)(2,1)S(1)}, bf16[2,256,256]{2,1,0:T(8,128)(2,1)S(1)}, u32[]{:S(2)}, u32[]{:S(2)}) collective-permute-start(bf16[2,256,256]{2,1,0:T(8,128)(2,1)S(1)} %collective-permute-done.5.rest_5_), channel_id=1, source_target_pairs={{4,8},{8,4},{1,5},{5,1},{6,10},{10,6},{3,7},{7,3},{12,16},{16,12},... | collective-permute-start | bytes 786440 | tf_op jit(solution)/shard_map/ppermute | solution.py:172
  58.6 15.6 %copy-start.6 = (bf16[256,256]{1,0:T(8,128)(2,1)S(1)}, bf16[256,256]{1,0:T(8,128)(2,1)}, u32[]{:S(2)}) copy-start(bf16[256,256]{1,0:T(8,128)(2,1)} %get-tuple-element.28.gate_ref) | copy-start | bytes 393220
  62.4 22.5 %copy-start.2 = (bf16[256,512]{1,0:T(8,128)(2,1)S(1)}, bf16[256,512]{1,0:T(8,128)(2,1)}, u32[]{:S(2)}) copy-start(bf16[256,512]{1,0:T(8,128)(2,1)} %constant.18.clone.high_ref) | copy-start | bytes 786436
  62.4 22.5 %copy-start.3 = (bf16[256,512]{1,0:T(8,128)(2,1)S(1)}, bf16[256,512]{1,0:T(8,128)(2,1)}, u32[]{:S(2)}) copy-start(bf16[256,512]{1,0:T(8,128)(2,1)} %constant.19.clone.low_ref) | copy-start | bytes 786436
  62.4 22.5 %copy-start.4 = (bf16[512,256]{1,0:T(8,128)(2,1)S(1)}, bf16[512,256]{1,0:T(8,128)(2,1)}, u32[]{:S(2)}) copy-start(bf16[512,256]{1,0:T(8,128)(2,1)} %constant.20.clone.ihigh_ref) | copy-start | bytes 786436
  62.5 22.5 %copy-start.5 = (bf16[512,256]{1,0:T(8,128)(2,1)S(1)}, bf16[512,256]{1,0:T(8,128)(2,1)}, u32[]{:S(2)}) copy-start(bf16[512,256]{1,0:T(8,128)(2,1)} %constant.21.clone.ilow_ref) | copy-start | bytes 786436

commit v3 on v2

--- a/solution.py
+++ b/solution.py
@@ -21,7 +21,7 @@
 
 def tables(block):
     angle = np.pi * (2 * np.arange(block) + 1)[None, :] / (2 * block)
-    sample = np.arange(2 * block)[:, None]
+    sample = np.arange(block)[:, None]
     forward = np.concatenate([np.cos(sample * angle), np.sin(sample * angle)], axis=1)
     lag = block - np.arange(block)[None, :]
     inverse = np.concatenate([np.cos(lag * angle.T), np.sin(lag * angle.T)], axis=0) / block
@@ -91,22 +91,24 @@
     out_ref[...] = (gate_ref[...].astype(F32) * pre_gate).astype(BF)
 
 
-def window_kernel(moved_ref, high_ref, low_ref, out_ref):
-    blocks, _, lanes, block = moved_ref.shape
-    rows = blocks * lanes
-    for which in range(2):
-        now = moved_ref[:, which].reshape(rows, block)
-        before = jnp.concatenate([jnp.zeros((lanes, block), BF), now[: rows - lanes]], axis=0)
-        window = jnp.concatenate([before, now], axis=1)
-        spectrum = dot(window, high_ref[...]) + dot(window, low_ref[...])
-        out_ref[which] = spectrum.reshape(blocks, lanes, 2 * block)
-
-
-def correlate_kernel(scale, grad_ref, window_ref, high_ref, low_ref, ihigh_ref, ilow_ref, out_ref, spec, cross):
+def correlate_kernel(scale, grad_ref, moved_ref, high_ref, low_ref, ihigh_ref, ilow_ref, out_ref, spec, window, cross):
     blocks, lanes, block = grad_ref.shape
     rows = blocks * lanes
-    grad = grad_ref[...].reshape(rows, block)
-    spec[...] = (dot(grad, high_ref[...]) + dot(grad, low_ref[...])).reshape(blocks, lanes, 2 * block)
+
+    def transform(value):
+        value = value.reshape(rows, block)
+        return dot(value, high_ref[...]) + dot(value, low_ref[...])
+
+    spec[...] = transform(grad_ref[...]).reshape(blocks, lanes, 2 * block)
+    sign = 1.0 - 2.0 * (lax.broadcasted_iota(jnp.int32, (1, block), 1) % 2).astype(F32)
+    none = jnp.zeros((lanes, block), F32)
+    for which in range(2):
+        now = transform(moved_ref[:, which])
+        re, im = now[:, :block], now[:, block:]
+        before_re = jnp.concatenate([none, re[: rows - lanes]], axis=0)
+        before_im = jnp.concatenate([none, im[: rows - lanes]], axis=0)
+        window[which, :, :, :block] = (before_re - sign * im).reshape(blocks, lanes, block)
+        window[which, :, :, block:] = (before_im + sign * re).reshape(blocks, lanes, block)
     zero = jnp.zeros((lanes, block), F32)
     for first in range(blocks):
 
@@ -114,7 +116,7 @@
             re, im = spec[first + d, :, :block], spec[first + d, :, block:]
             out = []
             for which in range(2):
-                wre, wim = window_ref[which, d, :, :block], window_ref[which, d, :, block:]
+                wre, wim = window[which, d, :, :block], window[which, d, :, block:]
                 out.append(totals[2 * which] + (re * wre + im * wim))
                 out.append(totals[2 * which + 1] + (re * wim - im * wre))
             return tuple(out)
@@ -173,7 +175,6 @@
 
     cores = [[i, i + 1] for i in range(0, members, 2)]
     far = swap(out_grad, [[i, i + 2] for i in range(0, members, 4)] + [[i + 1, i + 3] for i in range(0, members, 4)])
-    near = lax.all_gather(out_grad, "ch", axis=0, tiled=False, axis_index_groups=neighbours(0))
     columns, sequences = pl.pallas_call(
         columns_kernel,
         out_shape=[
@@ -184,23 +185,17 @@
         out_specs=whole(2),
         compiler_params=params(62 << 20),
     )(gate, filter_taps, conv_input)
+    local, columns, sequences = lax.optimization_barrier((out_grad, columns, sequences))
     sequences = lax.all_to_all(sequences, "ctx", split_axis=0, concat_axis=0, tiled=True)
-    windows = pl.pallas_call(
-        window_kernel,
-        out_shape=jax.ShapeDtypeStruct((2, blocks, lanes, 2 * block), F32),
-        in_specs=whole(3),
-        out_specs=whole(1)[0],
-        compiler_params=params(),
-    )(sequences, fhigh, flow)
+    near = lax.all_gather(local, "ch", axis=0, tiled=False, axis_index_groups=neighbours(0))
     lent = swap(out_weight, cores)
-    far, near, lent, columns = lax.optimization_barrier((far, near, lent, columns))
+    far, _, lent = lax.optimization_barrier((far, near, lent))
     far = lax.all_gather(far, "ch", axis=0, tiled=False, axis_index_groups=neighbours(0))
-    near, far = lax.optimization_barrier((near, far))
     parts = [near, far]
     for step in (1, 2, 3):
         near, far = swap(near, neighbours(step)), swap(far, neighbours(step))
         if step == 2:
-            near, windows = lax.optimization_barrier((near, windows))
+            near, sequences = lax.optimization_barrier((near, sequences))
         parts += [near, far]
 
     early, kept = pl.pallas_call(
@@ -244,9 +239,10 @@
         scratch_shapes=[
             pltpu.VMEM((blocks, lanes, 2 * block), F32),
             pltpu.VMEM((2, blocks, lanes, 2 * block), F32),
-        ],
-        compiler_params=params(),
-    )(moved, windows, fhigh[:block], flow[:block], ihigh, ilow)
+            pltpu.VMEM((2, blocks, lanes, 2 * block), F32),
+        ],
+        compiler_params=params(),
+    )(moved, sequences, fhigh, flow, ihigh, ilow)
     lags = lax.all_to_all(lags, "ctx", split_axis=0, concat_axis=0, tiled=True)
     return pl.pallas_call(
         finish_kernel,

time: 101 us -> 99.3 us (0.983)
  local copies, waits for them, and re-layouts: 2.12 us -> 0.03 us
    all_gather x1, blocking collectives: 9.91 us -> 6.36 us  [shards(): lax.all_gather(lend, 'ch', axis=0, tiled=False, axis_index_groups=cores)]
    all_to_all x1, blocking collectives: 10.7 us -> 13.1 us  [shards(): lax.all_to_all(gated.reshape(blocks, lanes, block), 'ctx', split_axis=0,...]
    unnamed x14 -> x10, local copies, waits for them, and re-layouts: 2.12 us -> 0.03 us
    all_gather x1, blocking collectives: 5.7 us -> 7.31 us  [shards(): lax.all_gather(far, 'ch', axis=0, tiled=False, axis_index_groups=neighbou...]
where the time goes in v3:
time: 99.3 us; the launch traced here: 98.8 us
  blocking collectives  51.5 us (52%)
  starting transfers between devices  33.1 us (33%)
  Pallas kernels  9.39 us (9%)
  waiting for transfers between devices  3.91 us (4%)
    ppermute x8, starting transfers between devices, swap(): lax.ppermute(value, 'ch', [(a, b) for pair in pairs for a, b in (pair, pa...  28.4 us
    all_to_all x1, blocking collectives, shards(): lax.all_to_all(gated.reshape(blocks, lanes, block), 'ctx', split_axis=0,...  13.1 us
    all_to_all x1, blocking collectives, shards(): lags = lax.all_to_all(lags, 'ctx', split_axis=0, concat_axis=0, tiled=True)  12.7 us
    all_gather x1, blocking collectives, shards(): lax.all_gather(local, 'ch', axis=0, tiled=False, axis_index_groups=neighb...  12 us
    all_gather x1, blocking collectives, shards(): lax.all_gather(far, 'ch', axis=0, tiled=False, axis_index_groups=neighbou...  7.31 us
    all_gather x1, blocking collectives, shards(): lax.all_gather(lend, 'ch', axis=0, tiled=False, axis_index_groups=cores)  6.36 us
    all_to_all x1, starting transfers between devices, shards(): lax.all_to_all(sequences, 'ctx', split_axis=0, concat_axis=0, tiled=True)  4.75 us
    pallas_call x1, Pallas kernels, shards(): pl.pallas_call(early_kernel, out_shape=[jax.ShapeDtypeStruct((2, channels...  3.82 us
  transfers between devices with their start and end apart: 9, of which 2 were waited for; matrix products, arithmetic and copies ran while one was open for 0% of the time, Pallas kernels for 6%

profile of v3, /device:TPU:1, one launch (start us, length us, event | category | flops | bytes accessed | tf_op | source)
XLA Modules:
  0.0 98.8 jit_solution(15843630965080516813)
XLA Ops:
  0.6 8.8 %collective-permute-start.1 = (bf16[256,8192]{1,0:T(8,128)(2,1)}, bf16[256,8192]{1,0:T(8,128)(2,1)}, u32[]{:S(2)}, u32[]{:S(2)}) collective-permute-start(bf16[256,8192]{1,0:T(8,128)(2,1)} %weight_ref.1), channel_id=1, source_target_pairs={{0,1},{1,0},{2,3},{3,2},{4,5},{5,4},{6,7},{7,6},{8,9},{9,8},{10,11... | collective-permute-start | bytes 12582920 | tf_op jit(solution)/shard_map/ppermute | solution.py:174
  9.4 2.1 %collective-permute-start = (bf16[256,256]{1,0:T(8,128)(2,1)}, bf16[256,256]{1,0:T(8,128)(2,1)S(1)}, u32[]{:S(2)}, u32[]{:S(2)}) collective-permute-start(bf16[256,256]{1,0:T(8,128)(2,1)} %param.11), channel_id=1, source_target_pairs={{0,2},{2,0},{4,6},{6,4},{8,10},{10,8},{12,14},{14,12},{16,18},{18,... | collective-permute-start | bytes 393224 | tf_op jit(solution)/shard_map/ppermute | solution.py:174
  11.5 1.9 %shard_map.104 = (bf16[256,256]{1,0:T(8,128)(2,1)}, bf16[16,2,16,256]{3,2,1,0:T(8,128)(2,1)}) custom-call(bf16[256,256]{1,0:T(8,128)(2,1)} %gate_ref.1, bf16[256,256]{1,0:T(8,128)(2,1)} %taps_ref.1, bf16[256,256]{1,0:T(8,128)(2,1)} %input_ref.1), custom_call_target="tpu_custom_call" | custom-call | tf_op jit(solution)/shard_map/pallas_call | solution.py:178
  13.4 12.0 %all-gather = bf16[512,256]{1,0:T(8,128)(2,1)S(1)} all-gather(bf16[256,256]{1,0:T(8,128)(2,1)} %param.11), channel_id=2, replica_groups={{0,4},{5,9},{2,6},{7,11},{8,12},{13,17},{10,14},{15,19},{16,20},{21,25}..., dimensions={0}, use_global_device_ids=true | all-gather | bytes 393216 | tf_op jit(solution)/shard_map/all_gather | solution.py:190
  25.5 1.9 %collective-permute-start.2 = (bf16[2,256,256]{2,1,0:T(8,128)(2,1)S(1)}, bf16[2,256,256]{2,1,0:T(8,128)(2,1)S(1)}, u32[]{:S(2)}, u32[]{:S(2)}) collective-permute-start(bf16[2,256,256]{2,1,0:T(8,128)(2,1)S(1)} %bitcast.6), channel_id=1, source_target_pairs={{4,8},{8,4},{1,5},{5,1},{6,10},{10,6},{3,7},{7,3},{12,16},{16,12},... | collective-permute-start | bytes 786440 | tf_op jit(solution)/shard_map/ppermute | solution.py:174
  27.4 0.0 collective-permute-done
  27.4 0.0 collective-permute-done.1.lent_ref
  27.4 7.3 %all-gather.1 = bf16[512,256]{1,0:T(8,128)(2,1)S(1)} all-gather(bf16[256,256]{1,0:T(8,128)(2,1)S(1)} %collective-permute-done), channel_id=3, replica_groups={{0,4},{5,9},{2,6},{7,11},{8,12},{13,17},{10,14},{15,19},{16,20},{21,25}..., dimensions={0}, use_global_device_ids=true | all-gather | bytes 393216 | tf_op jit(solution)/shard_map/all_gather | solution.py:193
  34.7 1.9 %collective-permute-start.3 = (bf16[2,256,256]{2,1,0:T(8,128)(2,1)S(1)}, bf16[2,256,256]{2,1,0:T(8,128)(2,1)S(1)}, u32[]{:S(2)}, u32[]{:S(2)}) collective-permute-start(bf16[2,256,256]{2,1,0:T(8,128)(2,1)S(1)} %bitcast.8), channel_id=1, source_target_pairs={{4,8},{8,4},{1,5},{5,1},{6,10},{10,6},{3,7},{7,3},{12,16},{16,12},... | collective-permute-start | bytes 786440 | tf_op jit(solution)/shard_map/ppermute | solution.py:174
  36.6 4.7 %all-to-all-start = ((bf16[16,2,16,256]{3,2,1,0:T(8,128)(2,1)}), bf16[16,2,16,256]{3,2,1,0:T(8,128)(2,1)S(1)}, u32[]{:S(2)}, u32[]{:S(2)}) async-start(bf16[16,2,16,256]{3,2,1,0:T(8,128)(2,1)} %get-tuple-element.20), calls=%async_computation | async-start | bytes 524288 | tf_op jit(solution)/shard_map/all_to_all | solution.py:189
  41.4 0.0 collective-permute-done.2.rest_2_
  41.4 4.7 %collective-permute-start.4 = (bf16[2,256,256]{2,1,0:T(8,128)(2,1)S(1)}, bf16[2,256,256]{2,1,0:T(8,128)(2,1)S(1)}, u32[]{:S(2)}, u32[]{:S(2)}) collective-permute-start(bf16[2,256,256]{2,1,0:T(8,128)(2,1)S(1)} %collective-permute-done.2.rest_2_), channel_id=1, source_target_pairs={{0,4},{4,0},{5,9},{9,5},{2,6},{6,2},{7,11},{11,7},{8,12},{12,8},{1... | collective-permute-start | bytes 786440 | tf_op jit(solution)/shard_map/ppermute | solution.py:174
  46.1 0.0 collective-permute-done.3.rest_3_
  46.1 1.9 %collective-permute-start.5 = (bf16[2,256,256]{2,1,0:T(8,128)(2,1)S(1)}, bf16[2,256,256]{2,1,0:T(8,128)(2,1)S(1)}, u32[]{:S(2)}, u32[]{:S(2)}) collective-permute-start(bf16[2,256,256]{2,1,0:T(8,128)(2,1)S(1)} %collective-permute-done.3.rest_3_), channel_id=1, source_target_pairs={{0,4},{4,0},{5,9},{9,5},{2,6},{6,2},{7,11},{11,7},{8,12},{12,8},{1... | collective-permute-start | bytes 786440 | tf_op jit(solution)/shard_map/ppermute | solution.py:174
  48.0 2.3 %all-to-all-done.moved_ref = bf16[16,2,16,256]{3,2,1,0:T(8,128)(2,1)S(1)} async-done(((bf16[16,2,16,256]{3,2,1,0:T(8,128)(2,1)}), bf16[16,2,16,256]{3,2,1,0:T(8,128)(2,1)S(1)}, u32[]{:S(2)}, u32[]{:S(2)}) %all-to-all-start) | async-done | bytes 262176 | tf_op jit(solution)/shard_map/all_to_all | solution.py:189
  50.3 0.0 collective-permute-done.4.rest_4_
  50.3 5.2 %collective-permute-start.6 = (bf16[2,256,256]{2,1,0:T(8,128)(2,1)S(1)}, bf16[2,256,256]{2,1,0:T(8,128)(2,1)S(1)}, u32[]{:S(2)}, u32[]{:S(2)}) collective-permute-start(bf16[2,256,256]{2,1,0:T(8,128)(2,1)S(1)} %collective-permute-done.4.rest_4_), channel_id=1, source_target_pairs={{4,8},{8,4},{1,5},{5,1},{6,10},{10,6},{3,7},{7,3},{12,16},{16,12},... | collective-permute-start | bytes 786440 | tf_op jit(solution)/shard_map/ppermute | solution.py:174
  55.5 0.0 collective-permute-done.5.rest_5_
  55.5 1.9 %collective-permute-start.7 = (bf16[2,256,256]{2,1,0:T(8,128)(2,1)S(1)}, bf16[2,256,256]{2,1,0:T(8,128)(2,1)S(1)}, u32[]{:S(2)}, u32[]{:S(2)}) collective-permute-start(bf16[2,256,256]{2,1,0:T(8,128)(2,1)S(1)} %collective-permute-done.5.rest_5_), channel_id=1, source_target_pairs={{4,8},{8,4},{1,5},{5,1},{6,10},{10,6},{3,7},{7,3},{12,16},{16,12},... | collective-permute-start | bytes 786440 | tf_op jit(solution)/shard_map/ppermute | solution.py:174
  57.4 0.0 copy-start.4
  57.4 3.8 %shard_map.105 = (f32[2,256,256]{2,1,0:T(8,128)S(1)}, bf16[2,256,1024]{2,1,0:T(8,128)(2,1)S(1)}) custom-call(s32[1]{0:T(128)} %bitcast.ch_ref, bf16[256,8192]{1,0:T(8,128)(2,1)} %weight_ref.1, bf16[256,8192]{1,0:T(8,128)(2,1)} %collective-permute-done.1.lent_ref, bf16[2,256,256]{2,1,0:T(8,128)(2,1)S(1)} %bitcast.7, bf16[2,256,256]{2,1,0:T(8,128)(2,1)S(1)} %bitcast.9, ...), custom_call_target="tpu_custom_call" | custom-call | flops 805306368 | bytes 8388608 | tf_op jit(solution)/shard_map/pallas_call | solution.py:201
  61.3 0.0 copy-start
  61.3 0.0 copy-start.1
  61.3 0.0 copy-start.2
  61.3 0.0 copy-start.3
  61.3 1.6 %collective-permute-done.7.far_ref = bf16[2,256,256]{2,1,0:T(8,128)(2,1)S(1)} collective-permute-done((bf16[2,256,256]{2,1,0:T(8,128)(2,1)S(1)}, bf16[2,256,256]{2,1,0:T(8,128)(2,1)S(1)}, u32[]{:S(2)}, u32[]{:S(2)}) %collective-permute-start.7) | collective-permute-done | bytes 262176 | tf_op jit(solution)/shard_map/ppermute | solution.py:174
  62.9 0.5 shard_map.106
  63.4 6.4 %all-gather.2 = f32[512,256]{1,0:T(8,128)S(1)} all-gather(f32[256,256]{1,0:T(8,128)S(1)} %get-tuple-element.25), channel_id=4, replica_groups={{0,1},{2,3},{4,5},{6,7},{8,9},{10,11},{12,13},{14,15},{16,17},{18,19},{..., dimensions={0}, use_global_device_ids=true | all-gather | bytes 786432 | tf_op jit(solution)/shard_map/all_gather | solution.py:224
  69.8 13.1 %all_to_all.15.grad_ref = bf16[16,16,256]{2,1,0:T(8,128)(2,1)S(1)} all-to-all(bf16[16,16,256]{2,1,0:T(8,128)(2,1)S(1)} %bitcast.10), channel_id=1, replica_groups=mesh['ctx'=16,'ch'=32] {'ctx'}, dimensions={0} | all-to-all | bytes 262144 | tf_op jit(solution)/shard_map/all_to_all | solution.py:233
  82.9 2.3 %shard_map.108 = bf16[16,2,16,256]{3,2,1,0:T(8,128)(2,1)S(1)} custom-call(bf16[16,16,256]{2,1,0:T(8,128)(2,1)S(1)} %all_to_all.15.grad_ref, bf16[16,2,16,256]{3,2,1,0:T(8,128)(2,1)S(1)} %all-to-all-done.moved_ref, bf16[256,512]{1,0:T(8,128)(2,1)S(1)} %copy-done, bf16[256,512]{1,0:T(8,128)(2,1)S(1)} %copy-done.1, bf16[512,256]{1,0:T(8,128)(2,1)S(1)} %copy-done.2, ...), custom_call_target="tpu_custom_call" | custom-call | tf_op jit(solution)/shard_map/pallas_call | solution.py:234
  85.2 12.7 %all_to_all.16.moved_ref = bf16[16,2,16,256]{3,2,1,0:T(8,128)(2,1)S(1)} all-to-all(bf16[16,2,16,256]{3,2,1,0:T(8,128)(2,1)S(1)} %shard_map.108), channel_id=1, replica_groups=mesh['ctx'=16,'ch'=32] {'ctx'}, dimensions={0} | all-to-all | bytes 524288 | tf_op jit(solution)/shard_map/all_to_all | solution.py:246
  97.9 0.9 shard_map.109
  (7 shorter events, 0.0 us)
Async XLA Ops:
  0.6 26.8 %collective-permute-start.1 = (bf16[256,8192]{1,0:T(8,128)(2,1)}, bf16[256,8192]{1,0:T(8,128)(2,1)}, u32[]{:S(2)}, u32[]{:S(2)}) collective-permute-start(bf16[256,8192]{1,0:T(8,128)(2,1)} %weight_ref.1), channel_id=1, source_target_pairs={{0,1},{1,0},{2,3},{3,2},{4,5},{5,4},{6,7},{7,6},{8,9},{9,8},{10,11... | collective-permute-start | bytes 12582920 | tf_op jit(solution)/shard_map/ppermute | solution.py:174
  9.4 18.0 %collective-permute-start = (bf16[256,256]{1,0:T(8,128)(2,1)}, bf16[256,256]{1,0:T(8,128)(2,1)S(1)}, u32[]{:S(2)}, u32[]{:S(2)}) collective-permute-start(bf16[256,256]{1,0:T(8,128)(2,1)} %param.11), channel_id=1, source_target_pairs={{0,2},{2,0},{4,6},{6,4},{8,10},{10,8},{12,14},{14,12},{16,18},{18,... | collective-permute-start | bytes 393224 | tf_op jit(solution)/shard_map/ppermute | solution.py:174
  25.5 15.9 %collective-permute-start.2 = (bf16[2,256,256]{2,1,0:T(8,128)(2,1)S(1)}, bf16[2,256,256]{2,1,0:T(8,128)(2,1)S(1)}, u32[]{:S(2)}, u32[]{:S(2)}) collective-permute-start(bf16[2,256,256]{2,1,0:T(8,128)(2,1)S(1)} %bitcast.6), channel_id=1, source_target_pairs={{4,8},{8,4},{1,5},{5,1},{6,10},{10,6},{3,7},{7,3},{12,16},{16,12},... | collective-permute-start | bytes 786440 | tf_op jit(solution)/shard_map/ppermute | solution.py:174
  34.7 11.4 %collective-permute-start.3 = (bf16[2,256,256]{2,1,0:T(8,128)(2,1)S(1)}, bf16[2,256,256]{2,1,0:T(8,128)(2,1)S(1)}, u32[]{:S(2)}, u32[]{:S(2)}) collective-permute-start(bf16[2,256,256]{2,1,0:T(8,128)(2,1)S(1)} %bitcast.8), channel_id=1, source_target_pairs={{4,8},{8,4},{1,5},{5,1},{6,10},{10,6},{3,7},{7,3},{12,16},{16,12},... | collective-permute-start | bytes 786440 | tf_op jit(solution)/shard_map/ppermute | solution.py:174
  36.6 13.7 %all-to-all-start = ((bf16[16,2,16,256]{3,2,1,0:T(8,128)(2,1)}), bf16[16,2,16,256]{3,2,1,0:T(8,128)(2,1)S(1)}, u32[]{:S(2)}, u32[]{:S(2)}) async-start(bf16[16,2,16,256]{3,2,1,0:T(8,128)(2,1)} %get-tuple-element.20), calls=%async_computation | async-start | bytes 524288 | tf_op jit(solution)/shard_map/all_to_all | solution.py:189
  41.4 8.9 %collective-permute-start.4 = (bf16[2,256,256]{2,1,0:T(8,128)(2,1)S(1)}, bf16[2,256,256]{2,1,0:T(8,128)(2,1)S(1)}, u32[]{:S(2)}, u32[]{:S(2)}) collective-permute-start(bf16[2,256,256]{2,1,0:T(8,128)(2,1)S(1)} %collective-permute-done.2.rest_2_), channel_id=1, source_target_pairs={{0,4},{4,0},{5,9},{9,5},{2,6},{6,2},{7,11},{11,7},{8,12},{12,8},{1... | collective-permute-start | bytes 786440 | tf_op jit(solution)/shard_map/ppermute | solution.py:174
  46.1 9.4 %collective-permute-start.5 = (bf16[2,256,256]{2,1,0:T(8,128)(2,1)S(1)}, bf16[2,256,256]{2,1,0:T(8,128)(2,1)S(1)}, u32[]{:S(2)}, u32[]{:S(2)}) collective-permute-start(bf16[2,256,256]{2,1,0:T(8,128)(2,1)S(1)} %collective-permute-done.3.rest_3_), channel_id=1, source_target_pairs={{0,4},{4,0},{5,9},{9,5},{2,6},{6,2},{7,11},{11,7},{8,12},{12,8},{1... | collective-permute-start | bytes 786440 | tf_op jit(solution)/shard_map/ppermute | solution.py:174
  50.3 11.0 %collective-permute-start.6 = (bf16[2,256,256]{2,1,0:T(8,128)(2,1)S(1)}, bf16[2,256,256]{2,1,0:T(8,128)(2,1)S(1)}, u32[]{:S(2)}, u32[]{:S(2)}) collective-permute-start(bf16[2,256,256]{2,1,0:T(8,128)(2,1)S(1)} %collective-permute-done.4.rest_4_), channel_id=1, source_target_pairs={{4,8},{8,4},{1,5},{5,1},{6,10},{10,6},{3,7},{7,3},{12,16},{16,12},... | collective-permute-start | bytes 786440 | tf_op jit(solution)/shard_map/ppermute | solution.py:174
  55.5 7.4 %collective-permute-start.7 = (bf16[2,256,256]{2,1,0:T(8,128)(2,1)S(1)}, bf16[2,256,256]{2,1,0:T(8,128)(2,1)S(1)}, u32[]{:S(2)}, u32[]{:S(2)}) collective-permute-start(bf16[2,256,256]{2,1,0:T(8,128)(2,1)S(1)} %collective-permute-done.5.rest_5_), channel_id=1, source_target_pairs={{4,8},{8,4},{1,5},{5,1},{6,10},{10,6},{3,7},{7,3},{12,16},{16,12},... | collective-permute-start | bytes 786440 | tf_op jit(solution)/shard_map/ppermute | solution.py:174
  57.4 12.3 %copy-start.4 = (bf16[256,256]{1,0:T(8,128)(2,1)S(1)}, bf16[256,256]{1,0:T(8,128)(2,1)}, u32[]{:S(2)}) copy-start(bf16[256,256]{1,0:T(8,128)(2,1)} %get-tuple-element.26.gate_ref) | copy-start | bytes 393220
  61.3 21.6 %copy-start = (bf16[256,512]{1,0:T(8,128)(2,1)S(1)}, bf16[256,512]{1,0:T(8,128)(2,1)}, u32[]{:S(2)}) copy-start(bf16[256,512]{1,0:T(8,128)(2,1)} %constant.12.clone.high_ref) | copy-start | bytes 786436
  61.3 21.6 %copy-start.1 = (bf16[256,512]{1,0:T(8,128)(2,1)S(1)}, bf16[256,512]{1,0:T(8,128)(2,1)}, u32[]{:S(2)}) copy-start(bf16[256,512]{1,0:T(8,128)(2,1)} %constant.13.clone.low_ref) | copy-start | bytes 786436
  61.3 21.6 %copy-start.2 = (bf16[512,256]{1,0:T(8,128)(2,1)S(1)}, bf16[512,256]{1,0:T(8,128)(2,1)}, u32[]{:S(2)}) copy-start(bf16[512,256]{1,0:T(8,128)(2,1)} %constant.14.clone.ihigh_ref) | copy-start | bytes 786436
  61.3 21.6 %copy-start.3 = (bf16[512,256]{1,0:T(8,128)(2,1)S(1)}, bf16[512,256]{1,0:T(8,128)(2,1)}, u32[]{:S(2)}) copy-start(bf16[512,256]{1,0:T(8,128)(2,1)} %constant.15.clone.ilow_ref) | copy-start | bytes 786436

commit v4 on v3

--- a/solution.py
+++ b/solution.py
@@ -174,7 +174,6 @@
         return lax.ppermute(value, "ch", [(a, b) for pair in pairs for a, b in (pair, pair[::-1])])
 
     cores = [[i, i + 1] for i in range(0, members, 2)]
-    far = swap(out_grad, [[i, i + 2] for i in range(0, members, 4)] + [[i + 1, i + 3] for i in range(0, members, 4)])
     columns, sequences = pl.pallas_call(
         columns_kernel,
         out_shape=[
@@ -185,16 +184,15 @@
         out_specs=whole(2),
         compiler_params=params(62 << 20),
     )(gate, filter_taps, conv_input)
-    local, columns, sequences = lax.optimization_barrier((out_grad, columns, sequences))
     sequences = lax.all_to_all(sequences, "ctx", split_axis=0, concat_axis=0, tiled=True)
-    near = lax.all_gather(local, "ch", axis=0, tiled=False, axis_index_groups=neighbours(0))
+    near = lax.all_gather(out_grad, "ch", axis=0, tiled=False, axis_index_groups=neighbours(0))
     lent = swap(out_weight, cores)
-    far, _, lent = lax.optimization_barrier((far, near, lent))
-    far = lax.all_gather(far, "ch", axis=0, tiled=False, axis_index_groups=neighbours(0))
+    sides = [[spot(z, 0, c), spot(z, 1, c)] for z in range(8) for c in range(2)]
+    far = swap(near, sides)
     parts = [near, far]
     for step in (1, 2, 3):
         near, far = swap(near, neighbours(step)), swap(far, neighbours(step))
-        if step == 2:
+        if step == 1:
             near, sequences = lax.optimization_barrier((near, sequences))
         parts += [near, far]
 

time: 99.3 us -> 98.5 us (level)
  blocking collectives: 51.5 us -> 37.3 us
  waiting for transfers between devices: 3.91 us -> 10.8 us
  starting transfers between devices: 33.1 us -> 39.6 us
    all_gather x2 -> x1, blocking collectives: 19.3 us -> 6.67 us  [shards(): lax.all_gather(out_grad, 'ch', axis=0, tiled=False, axis_index_groups=nei...]
    ppermute x8, waiting for transfers between devices: 1.59 us -> 9.41 us  [swap(): lax.ppermute(value, 'ch', [(a, b) for pair in pairs for a, b in (pair, pa...]
    ppermute x8, starting transfers between devices: 28.4 us -> 35.1 us  [swap(): lax.ppermute(value, 'ch', [(a, b) for pair in pairs for a, b in (pair, pa...]
    all_gather x1, blocking collectives: 6.36 us -> 4.76 us  [shards(): lax.all_gather(lend, 'ch', axis=0, tiled=False, axis_index_groups=cores)]
  transfers between devices with their start and end apart: 9 -> 9, of which waited for: 2 -> 6; matrix products, arithmetic and copies ran while one was open for 0% -> 0% of each run, Pallas kernels for 6% -> 6%
where the time goes in v4:
time: 98.5 us; the launch traced here: 97.9 us
  starting transfers between devices  39.6 us (40%)
  blocking collectives  37.3 us (38%)
  waiting for transfers between devices  10.8 us (11%)
  Pallas kernels  9.39 us (10%)
    ppermute x8, starting transfers between devices, swap(): lax.ppermute(value, 'ch', [(a, b) for pair in pairs for a, b in (pair, pa...  35.1 us
    all_to_all x1, blocking collectives, shards(): lax.all_to_all(gated.reshape(blocks, lanes, block), 'ctx', split_axis=0,...  13.1 us
    all_to_all x1, blocking collectives, shards(): lags = lax.all_to_all(lags, 'ctx', split_axis=0, concat_axis=0, tiled=True)  12.7 us
    ppermute x8, waiting for transfers between devices, swap(): lax.ppermute(value, 'ch', [(a, b) for pair in pairs for a, b in (pair, pa...  9.41 us
    all_gather x1, blocking collectives, shards(): lax.all_gather(out_grad, 'ch', axis=0, tiled=False, axis_index_groups=nei...  6.67 us
    all_gather x1, blocking collectives, shards(): lax.all_gather(lend, 'ch', axis=0, tiled=False, axis_index_groups=cores)  4.76 us
    all_to_all x1, starting transfers between devices, shards(): lax.all_to_all(sequences, 'ctx', split_axis=0, concat_axis=0, tiled=True)  4.47 us
    pallas_call x1, Pallas kernels, shards(): pl.pallas_call(early_kernel, out_shape=[jax.ShapeDtypeStruct((2, channels...  3.82 us
  transfers between devices with their start and end apart: 9, of which 6 were waited for; matrix products, arithmetic and copies ran while one was open for 0% of the time, Pallas kernels for 6%

profile of v4, /device:TPU:1, one launch (start us, length us, event | category | flops | bytes accessed | tf_op | source)
XLA Modules:
  0.0 97.9 jit_solution(17068456767289339542)
XLA Ops:
  0.6 8.8 %collective-permute-start = (bf16[256,8192]{1,0:T(8,128)(2,1)}, bf16[256,8192]{1,0:T(8,128)(2,1)}, u32[]{:S(2)}, u32[]{:S(2)}) collective-permute-start(bf16[256,8192]{1,0:T(8,128)(2,1)} %weight_ref.1), channel_id=1, source_target_pairs={{0,1},{1,0},{2,3},{3,2},{4,5},{5,4},{6,7},{7,6},{8,9},{9,8},{10,11... | collective-permute-start | bytes 12582920 | tf_op jit(solution)/shard_map/ppermute | solution.py:174
  9.4 6.7 %all-gather = bf16[512,256]{1,0:T(8,128)(2,1)S(1)} all-gather(bf16[256,256]{1,0:T(8,128)(2,1)} %param.11), channel_id=2, replica_groups={{0,4},{5,9},{2,6},{7,11},{8,12},{13,17},{10,14},{15,19},{16,20},{21,25}..., dimensions={0}, use_global_device_ids=true | all-gather | bytes 393216 | tf_op jit(solution)/shard_map/all_gather | solution.py:188
  16.1 7.4 %collective-permute-start.1 = (bf16[2,256,256]{2,1,0:T(8,128)(2,1)S(1)}, bf16[2,256,256]{2,1,0:T(8,128)(2,1)S(1)}, u32[]{:S(2)}, u32[]{:S(2)}) collective-permute-start(bf16[2,256,256]{2,1,0:T(8,128)(2,1)S(1)} %bitcast.5), channel_id=1, source_target_pairs={{0,2},{2,0},{1,3},{3,1},{4,6},{6,4},{5,7},{7,5},{8,10},{10,8},{9,1... | collective-permute-start | bytes 786440 | tf_op jit(solution)/shard_map/ppermute | solution.py:174
  23.6 1.9 %shard_map.104 = (bf16[256,256]{1,0:T(8,128)(2,1)}, bf16[16,2,16,256]{3,2,1,0:T(8,128)(2,1)}) custom-call(bf16[256,256]{1,0:T(8,128)(2,1)} %gate_ref.1, bf16[256,256]{1,0:T(8,128)(2,1)} %taps_ref.1, bf16[256,256]{1,0:T(8,128)(2,1)} %input_ref.1), custom_call_target="tpu_custom_call" | custom-call | tf_op jit(solution)/shard_map/pallas_call | solution.py:177
  25.5 4.5 %all-to-all-start = ((bf16[16,2,16,256]{3,2,1,0:T(8,128)(2,1)}), bf16[16,2,16,256]{3,2,1,0:T(8,128)(2,1)S(1)}, u32[]{:S(2)}, u32[]{:S(2)}) async-start(bf16[16,2,16,256]{3,2,1,0:T(8,128)(2,1)} %get-tuple-element.10), calls=%async_computation | async-start | bytes 524288 | tf_op jit(solution)/shard_map/all_to_all | solution.py:187
  29.9 1.9 %collective-permute-start.2 = (bf16[2,256,256]{2,1,0:T(8,128)(2,1)S(1)}, bf16[2,256,256]{2,1,0:T(8,128)(2,1)S(1)}, u32[]{:S(2)}, u32[]{:S(2)}) collective-permute-start(bf16[2,256,256]{2,1,0:T(8,128)(2,1)S(1)} %bitcast.6), channel_id=1, source_target_pairs={{4,8},{8,4},{1,5},{5,1},{6,10},{10,6},{3,7},{7,3},{12,16},{16,12},... | collective-permute-start | bytes 786440 | tf_op jit(solution)/shard_map/ppermute | solution.py:174
  31.9 1.3 %collective-permute-done.1.rest_1_ = bf16[2,256,256]{2,1,0:T(8,128)(2,1)S(1)} collective-permute-done((bf16[2,256,256]{2,1,0:T(8,128)(2,1)S(1)}, bf16[2,256,256]{2,1,0:T(8,128)(2,1)S(1)}, u32[]{:S(2)}, u32[]{:S(2)}) %collective-permute-start.1) | collective-permute-done | bytes 262176 | tf_op jit(solution)/shard_map/ppermute | solution.py:174
  33.1 2.1 %collective-permute-start.3 = (bf16[2,256,256]{2,1,0:T(8,128)(2,1)S(1)}, bf16[2,256,256]{2,1,0:T(8,128)(2,1)S(1)}, u32[]{:S(2)}, u32[]{:S(2)}) collective-permute-start(bf16[2,256,256]{2,1,0:T(8,128)(2,1)S(1)} %collective-permute-done.1.rest_1_), channel_id=1, source_target_pairs={{4,8},{8,4},{1,5},{5,1},{6,10},{10,6},{3,7},{7,3},{12,16},{16,12},... | collective-permute-start | bytes 786440 | tf_op jit(solution)/shard_map/ppermute | solution.py:174
  35.2 2.1 %collective-permute-done.2.rest_2_ = bf16[2,256,256]{2,1,0:T(8,128)(2,1)S(1)} collective-permute-done((bf16[2,256,256]{2,1,0:T(8,128)(2,1)S(1)}, bf16[2,256,256]{2,1,0:T(8,128)(2,1)S(1)}, u32[]{:S(2)}, u32[]{:S(2)}) %collective-permute-start.2) | collective-permute-done | bytes 262176 | tf_op jit(solution)/shard_map/ppermute | solution.py:174
  37.3 1.4 %all-to-all-done.moved_ref = bf16[16,2,16,256]{3,2,1,0:T(8,128)(2,1)S(1)} async-done(((bf16[16,2,16,256]{3,2,1,0:T(8,128)(2,1)}), bf16[16,2,16,256]{3,2,1,0:T(8,128)(2,1)S(1)}, u32[]{:S(2)}, u32[]{:S(2)}) %all-to-all-start) | async-done | bytes 262176 | tf_op jit(solution)/shard_map/all_to_all | solution.py:187
  38.8 9.1 %collective-permute-start.4 = (bf16[2,256,256]{2,1,0:T(8,128)(2,1)S(1)}, bf16[2,256,256]{2,1,0:T(8,128)(2,1)S(1)}, u32[]{:S(2)}, u32[]{:S(2)}) collective-permute-start(bf16[2,256,256]{2,1,0:T(8,128)(2,1)S(1)} %collective-permute-done.2.rest_2_), channel_id=1, source_target_pairs={{0,4},{4,0},{5,9},{9,5},{2,6},{6,2},{7,11},{11,7},{8,12},{12,8},{1... | collective-permute-start | bytes 786440 | tf_op jit(solution)/shard_map/ppermute | solution.py:174
  47.9 0.0 collective-permute-done.3.rest_3_
  47.9 1.9 %collective-permute-start.5 = (bf16[2,256,256]{2,1,0:T(8,128)(2,1)S(1)}, bf16[2,256,256]{2,1,0:T(8,128)(2,1)S(1)}, u32[]{:S(2)}, u32[]{:S(2)}) collective-permute-start(bf16[2,256,256]{2,1,0:T(8,128)(2,1)S(1)} %collective-permute-done.3.rest_3_), channel_id=1, source_target_pairs={{0,4},{4,0},{5,9},{9,5},{2,6},{6,2},{7,11},{11,7},{8,12},{12,8},{1... | collective-permute-start | bytes 786440 | tf_op jit(solution)/shard_map/ppermute | solution.py:174
  49.8 1.8 %collective-permute-done.4.rest_4_ = bf16[2,256,256]{2,1,0:T(8,128)(2,1)S(1)} collective-permute-done((bf16[2,256,256]{2,1,0:T(8,128)(2,1)S(1)}, bf16[2,256,256]{2,1,0:T(8,128)(2,1)S(1)}, u32[]{:S(2)}, u32[]{:S(2)}) %collective-permute-start.4) | collective-permute-done | bytes 262176 | tf_op jit(solution)/shard_map/ppermute | solution.py:174
  51.6 1.9 %collective-permute-start.6 = (bf16[2,256,256]{2,1,0:T(8,128)(2,1)S(1)}, bf16[2,256,256]{2,1,0:T(8,128)(2,1)S(1)}, u32[]{:S(2)}, u32[]{:S(2)}) collective-permute-start(bf16[2,256,256]{2,1,0:T(8,128)(2,1)S(1)} %collective-permute-done.4.rest_4_), channel_id=1, source_target_pairs={{4,8},{8,4},{1,5},{5,1},{6,10},{10,6},{3,7},{7,3},{12,16},{16,12},... | collective-permute-start | bytes 786440 | tf_op jit(solution)/shard_map/ppermute | solution.py:174
  53.5 2.7 %collective-permute-done.5.rest_5_ = bf16[2,256,256]{2,1,0:T(8,128)(2,1)S(1)} collective-permute-done((bf16[2,256,256]{2,1,0:T(8,128)(2,1)S(1)}, bf16[2,256,256]{2,1,0:T(8,128)(2,1)S(1)}, u32[]{:S(2)}, u32[]{:S(2)}) %collective-permute-start.5) | collective-permute-done | bytes 262176 | tf_op jit(solution)/shard_map/ppermute | solution.py:174
  56.2 1.9 %collective-permute-start.7 = (bf16[2,256,256]{2,1,0:T(8,128)(2,1)S(1)}, bf16[2,256,256]{2,1,0:T(8,128)(2,1)S(1)}, u32[]{:S(2)}, u32[]{:S(2)}) collective-permute-start(bf16[2,256,256]{2,1,0:T(8,128)(2,1)S(1)} %collective-permute-done.5.rest_5_), channel_id=1, source_target_pairs={{4,8},{8,4},{1,5},{5,1},{6,10},{10,6},{3,7},{7,3},{12,16},{16,12},... | collective-permute-start | bytes 786440 | tf_op jit(solution)/shard_map/ppermute | solution.py:174
  58.1 0.0 collective-permute-done.lent_ref
  58.1 0.0 copy-start.4
  58.2 3.8 %shard_map.105 = (f32[2,256,256]{2,1,0:T(8,128)S(1)}, bf16[2,256,1024]{2,1,0:T(8,128)(2,1)S(1)}) custom-call(s32[1]{0:T(128)} %bitcast.ch_ref, bf16[256,8192]{1,0:T(8,128)(2,1)} %weight_ref.1, bf16[256,8192]{1,0:T(8,128)(2,1)} %collective-permute-done.lent_ref, bf16[2,256,256]{2,1,0:T(8,128)(2,1)S(1)} %bitcast.7, ...), custom_call_target="tpu_custom_call" | custom-call | flops 805306368 | bytes 8388608 | tf_op jit(solution)/shard_map/pallas_call | solution.py:199
  62.0 0.0 copy-start
  62.0 0.0 copy-start.1
  62.0 0.0 copy-start.2
  62.0 0.0 copy-start.3
  62.0 0.0 collective-permute-done.6.near_ref
  62.1 1.6 %collective-permute-done.7.far_ref = bf16[2,256,256]{2,1,0:T(8,128)(2,1)S(1)} collective-permute-done((bf16[2,256,256]{2,1,0:T(8,128)(2,1)S(1)}, bf16[2,256,256]{2,1,0:T(8,128)(2,1)S(1)}, u32[]{:S(2)}, u32[]{:S(2)}) %collective-permute-start.7) | collective-permute-done | bytes 262176 | tf_op jit(solution)/shard_map/ppermute | solution.py:174
  63.6 0.5 shard_map.106
  64.1 4.8 %all-gather.1 = f32[512,256]{1,0:T(8,128)S(1)} all-gather(f32[256,256]{1,0:T(8,128)S(1)} %get-tuple-element.15), channel_id=3, replica_groups={{0,1},{2,3},{4,5},{6,7},{8,9},{10,11},{12,13},{14,15},{16,17},{18,19},{..., dimensions={0}, use_global_device_ids=true | all-gather | bytes 786432 | tf_op jit(solution)/shard_map/all_gather | solution.py:222
  68.9 13.1 %all_to_all.15.grad_ref = bf16[16,16,256]{2,1,0:T(8,128)(2,1)S(1)} all-to-all(bf16[16,16,256]{2,1,0:T(8,128)(2,1)S(1)} %bitcast.8), channel_id=1, replica_groups=mesh['ctx'=16,'ch'=32] {'ctx'}, dimensions={0} | all-to-all | bytes 262144 | tf_op jit(solution)/shard_map/all_to_all | solution.py:231
  82.0 2.3 %shard_map.108 = bf16[16,2,16,256]{3,2,1,0:T(8,128)(2,1)S(1)} custom-call(bf16[16,16,256]{2,1,0:T(8,128)(2,1)S(1)} %all_to_all.15.grad_ref, bf16[16,2,16,256]{3,2,1,0:T(8,128)(2,1)S(1)} %all-to-all-done.moved_ref, bf16[256,512]{1,0:T(8,128)(2,1)S(1)} %copy-done, bf16[256,512]{1,0:T(8,128)(2,1)S(1)} %copy-done.1, bf16[512,256]{1,0:T(8,128)(2,1)S(1)} %copy-done.2, ...), custom_call_target="tpu_custom_call" | custom-call | tf_op jit(solution)/shard_map/pallas_call | solution.py:232
  84.3 12.7 %all_to_all.16.moved_ref = bf16[16,2,16,256]{3,2,1,0:T(8,128)(2,1)S(1)} all-to-all(bf16[16,2,16,256]{3,2,1,0:T(8,128)(2,1)S(1)} %shard_map.108), channel_id=1, replica_groups=mesh['ctx'=16,'ch'=32] {'ctx'}, dimensions={0} | all-to-all | bytes 524288 | tf_op jit(solution)/shard_map/all_to_all | solution.py:244
  97.0 0.9 shard_map.109
  (6 shorter events, 0.0 us)
Async XLA Ops:
  0.6 57.5 %collective-permute-start = (bf16[256,8192]{1,0:T(8,128)(2,1)}, bf16[256,8192]{1,0:T(8,128)(2,1)}, u32[]{:S(2)}, u32[]{:S(2)}) collective-permute-start(bf16[256,8192]{1,0:T(8,128)(2,1)} %weight_ref.1), channel_id=1, source_target_pairs={{0,1},{1,0},{2,3},{3,2},{4,5},{5,4},{6,7},{7,6},{8,9},{9,8},{10,11... | collective-permute-start | bytes 12582920 | tf_op jit(solution)/shard_map/ppermute | solution.py:174
  16.1 17.0 %collective-permute-start.1 = (bf16[2,256,256]{2,1,0:T(8,128)(2,1)S(1)}, bf16[2,256,256]{2,1,0:T(8,128)(2,1)S(1)}, u32[]{:S(2)}, u32[]{:S(2)}) collective-permute-start(bf16[2,256,256]{2,1,0:T(8,128)(2,1)S(1)} %bitcast.5), channel_id=1, source_target_pairs={{0,2},{2,0},{1,3},{3,1},{4,6},{6,4},{5,7},{7,5},{8,10},{10,8},{9,1... | collective-permute-start | bytes 786440 | tf_op jit(solution)/shard_map/ppermute | solution.py:174
  25.5 13.3 %all-to-all-start = ((bf16[16,2,16,256]{3,2,1,0:T(8,128)(2,1)}), bf16[16,2,16,256]{3,2,1,0:T(8,128)(2,1)S(1)}, u32[]{:S(2)}, u32[]{:S(2)}) async-start(bf16[16,2,16,256]{3,2,1,0:T(8,128)(2,1)} %get-tuple-element.10), calls=%async_computation | async-start | bytes 524288 | tf_op jit(solution)/shard_map/all_to_all | solution.py:187
  29.9 7.4 %collective-permute-start.2 = (bf16[2,256,256]{2,1,0:T(8,128)(2,1)S(1)}, bf16[2,256,256]{2,1,0:T(8,128)(2,1)S(1)}, u32[]{:S(2)}, u32[]{:S(2)}) collective-permute-start(bf16[2,256,256]{2,1,0:T(8,128)(2,1)S(1)} %bitcast.6), channel_id=1, source_target_pairs={{4,8},{8,4},{1,5},{5,1},{6,10},{10,6},{3,7},{7,3},{12,16},{16,12},... | collective-permute-start | bytes 786440 | tf_op jit(solution)/shard_map/ppermute | solution.py:174
  33.1 14.8 %collective-permute-start.3 = (bf16[2,256,256]{2,1,0:T(8,128)(2,1)S(1)}, bf16[2,256,256]{2,1,0:T(8,128)(2,1)S(1)}, u32[]{:S(2)}, u32[]{:S(2)}) collective-permute-start(bf16[2,256,256]{2,1,0:T(8,128)(2,1)S(1)} %collective-permute-done.1.rest_1_), channel_id=1, source_target_pairs={{4,8},{8,4},{1,5},{5,1},{6,10},{10,6},{3,7},{7,3},{12,16},{16,12},... | collective-permute-start | bytes 786440 | tf_op jit(solution)/shard_map/ppermute | solution.py:174
  38.8 12.9 %collective-permute-start.4 = (bf16[2,256,256]{2,1,0:T(8,128)(2,1)S(1)}, bf16[2,256,256]{2,1,0:T(8,128)(2,1)S(1)}, u32[]{:S(2)}, u32[]{:S(2)}) collective-permute-start(bf16[2,256,256]{2,1,0:T(8,128)(2,1)S(1)} %collective-permute-done.2.rest_2_), channel_id=1, source_target_pairs={{0,4},{4,0},{5,9},{9,5},{2,6},{6,2},{7,11},{11,7},{8,12},{12,8},{1... | collective-permute-start | bytes 786440 | tf_op jit(solution)/shard_map/ppermute | solution.py:174
  47.9 8.3 %collective-permute-start.5 = (bf16[2,256,256]{2,1,0:T(8,128)(2,1)S(1)}, bf16[2,256,256]{2,1,0:T(8,128)(2,1)S(1)}, u32[]{:S(2)}, u32[]{:S(2)}) collective-permute-start(bf16[2,256,256]{2,1,0:T(8,128)(2,1)S(1)} %collective-permute-done.3.rest_3_), channel_id=1, source_target_pairs={{0,4},{4,0},{5,9},{9,5},{2,6},{6,2},{7,11},{11,7},{8,12},{12,8},{1... | collective-permute-start | bytes 786440 | tf_op jit(solution)/shard_map/ppermute | solution.py:174
  51.6 10.4 %collective-permute-start.6 = (bf16[2,256,256]{2,1,0:T(8,128)(2,1)S(1)}, bf16[2,256,256]{2,1,0:T(8,128)(2,1)S(1)}, u32[]{:S(2)}, u32[]{:S(2)}) collective-permute-start(bf16[2,256,256]{2,1,0:T(8,128)(2,1)S(1)} %collective-permute-done.4.rest_4_), channel_id=1, source_target_pairs={{4,8},{8,4},{1,5},{5,1},{6,10},{10,6},{3,7},{7,3},{12,16},{16,12},... | collective-permute-start | bytes 786440 | tf_op jit(solution)/shard_map/ppermute | solution.py:174
  56.2 7.4 %collective-permute-start.7 = (bf16[2,256,256]{2,1,0:T(8,128)(2,1)S(1)}, bf16[2,256,256]{2,1,0:T(8,128)(2,1)S(1)}, u32[]{:S(2)}, u32[]{:S(2)}) collective-permute-start(bf16[2,256,256]{2,1,0:T(8,128)(2,1)S(1)} %collective-permute-done.5.rest_5_), channel_id=1, source_target_pairs={{4,8},{8,4},{1,5},{5,1},{6,10},{10,6},{3,7},{7,3},{12,16},{16,12},... | collective-permute-start | bytes 786440 | tf_op jit(solution)/shard_map/ppermute | solution.py:174
  58.1 10.7 %copy-start.4 = (bf16[256,256]{1,0:T(8,128)(2,1)S(1)}, bf16[256,256]{1,0:T(8,128)(2,1)}, u32[]{:S(2)}) copy-start(bf16[256,256]{1,0:T(8,128)(2,1)} %get-tuple-element.16.gate_ref) | copy-start | bytes 393220
  62.0 20.0 %copy-start = (bf16[256,512]{1,0:T(8,128)(2,1)S(1)}, bf16[256,512]{1,0:T(8,128)(2,1)}, u32[]{:S(2)}) copy-start(bf16[256,512]{1,0:T(8,128)(2,1)} %constant.12.clone.high_ref) | copy-start | bytes 786436
  62.0 20.0 %copy-start.1 = (bf16[256,512]{1,0:T(8,128)(2,1)S(1)}, bf16[256,512]{1,0:T(8,128)(2,1)}, u32[]{:S(2)}) copy-start(bf16[256,512]{1,0:T(8,128)(2,1)} %constant.13.clone.low_ref) | copy-start | bytes 786436
  62.0 20.0 %copy-start.2 = (bf16[512,256]{1,0:T(8,128)(2,1)S(1)}, bf16[512,256]{1,0:T(8,128)(2,1)}, u32[]{:S(2)}) copy-start(bf16[512,256]{1,0:T(8,128)(2,1)} %constant.14.clone.ihigh_ref) | copy-start | bytes 786436
  62.0 20.0 %copy-start.3 = (bf16[512,256]{1,0:T(8,128)(2,1)S(1)}, bf16[512,256]{1,0:T(8,128)(2,1)}, u32[]{:S(2)}) copy-start(bf16[512,256]{1,0:T(8,128)(2,1)} %constant.15.clone.ilow_ref) | copy-start | bytes 786436

commit v5 on v4

--- a/solution.py
+++ b/solution.py
@@ -191,7 +191,8 @@
     far = swap(near, sides)
     parts = [near, far]
     for step in (1, 2, 3):
-        near, far = swap(near, neighbours(step)), swap(far, neighbours(step))
+        far = swap(far, neighbours(step))
+        near = swap(near, neighbours(step))
         if step == 1:
             near, sequences = lax.optimization_barrier((near, sequences))
         parts += [near, far]

time: 98.5 us -> 98.5 us (level)
  no operation moved by 1% of the time
where the time goes in v5:
time: 98.5 us; the launch traced here: 97.9 us
  starting transfers between devices  39.6 us (40%)
  blocking collectives  37.3 us (38%)
  waiting for transfers between devices  10.8 us (11%)
  Pallas kernels  9.39 us (10%)
    ppermute x8, starting transfers between devices, swap(): lax.ppermute(value, 'ch', [(a, b) for pair in pairs for a, b in (pair, pa...  35.1 us
    all_to_all x1, blocking collectives, shards(): lax.all_to_all(gated.reshape(blocks, lanes, block), 'ctx', split_axis=0,...  13.1 us
    all_to_all x1, blocking collectives, shards(): lags = lax.all_to_all(lags, 'ctx', split_axis=0, concat_axis=0, tiled=True)  12.7 us
    ppermute x8, waiting for transfers between devices, swap(): lax.ppermute(value, 'ch', [(a, b) for pair in pairs for a, b in (pair, pa...  9.41 us
    all_gather x1, blocking collectives, shards(): lax.all_gather(out_grad, 'ch', axis=0, tiled=False, axis_index_groups=nei...  6.67 us
    all_gather x1, blocking collectives, shards(): lax.all_gather(lend, 'ch', axis=0, tiled=False, axis_index_groups=cores)  4.76 us
    all_to_all x1, starting transfers between devices, shards(): lax.all_to_all(sequences, 'ctx', split_axis=0, concat_axis=0, tiled=True)  4.47 us
    pallas_call x1, Pallas kernels, shards(): pl.pallas_call(early_kernel, out_shape=[jax.ShapeDtypeStruct((2, channels...  3.82 us
  transfers between devices with their start and end apart: 9, of which 6 were waited for; matrix products, arithmetic and copies ran while one was open for 0% of the time, Pallas kernels for 6%

profile of v5, /device:TPU:1, one launch (start us, length us, event | category | flops | bytes accessed | tf_op | source)
XLA Modules:
  0.0 97.9 jit_solution(17068456767289339542)
XLA Ops:
  0.6 8.8 %collective-permute-start = (bf16[256,8192]{1,0:T(8,128)(2,1)}, bf16[256,8192]{1,0:T(8,128)(2,1)}, u32[]{:S(2)}, u32[]{:S(2)}) collective-permute-start(bf16[256,8192]{1,0:T(8,128)(2,1)} %weight_ref.1), channel_id=1, source_target_pairs={{0,1},{1,0},{2,3},{3,2},{4,5},{5,4},{6,7},{7,6},{8,9},{9,8},{10,11... | collective-permute-start | bytes 12582920 | tf_op jit(solution)/shard_map/ppermute | solution.py:174
  9.4 6.7 %all-gather = bf16[512,256]{1,0:T(8,128)(2,1)S(1)} all-gather(bf16[256,256]{1,0:T(8,128)(2,1)} %param.11), channel_id=2, replica_groups={{0,4},{5,9},{2,6},{7,11},{8,12},{13,17},{10,14},{15,19},{16,20},{21,25}..., dimensions={0}, use_global_device_ids=true | all-gather | bytes 393216 | tf_op jit(solution)/shard_map/all_gather | solution.py:188
  16.1 7.4 %collective-permute-start.1 = (bf16[2,256,256]{2,1,0:T(8,128)(2,1)S(1)}, bf16[2,256,256]{2,1,0:T(8,128)(2,1)S(1)}, u32[]{:S(2)}, u32[]{:S(2)}) collective-permute-start(bf16[2,256,256]{2,1,0:T(8,128)(2,1)S(1)} %bitcast.5), channel_id=1, source_target_pairs={{0,2},{2,0},{1,3},{3,1},{4,6},{6,4},{5,7},{7,5},{8,10},{10,8},{9,1... | collective-permute-start | bytes 786440 | tf_op jit(solution)/shard_map/ppermute | solution.py:174
  23.6 1.9 %shard_map.104 = (bf16[256,256]{1,0:T(8,128)(2,1)}, bf16[16,2,16,256]{3,2,1,0:T(8,128)(2,1)}) custom-call(bf16[256,256]{1,0:T(8,128)(2,1)} %gate_ref.1, bf16[256,256]{1,0:T(8,128)(2,1)} %taps_ref.1, bf16[256,256]{1,0:T(8,128)(2,1)} %input_ref.1), custom_call_target="tpu_custom_call" | custom-call | tf_op jit(solution)/shard_map/pallas_call | solution.py:177
  25.5 4.5 %all-to-all-start = ((bf16[16,2,16,256]{3,2,1,0:T(8,128)(2,1)}), bf16[16,2,16,256]{3,2,1,0:T(8,128)(2,1)S(1)}, u32[]{:S(2)}, u32[]{:S(2)}) async-start(bf16[16,2,16,256]{3,2,1,0:T(8,128)(2,1)} %get-tuple-element.10), calls=%async_computation | async-start | bytes 524288 | tf_op jit(solution)/shard_map/all_to_all | solution.py:187
  29.9 1.9 %collective-permute-start.2 = (bf16[2,256,256]{2,1,0:T(8,128)(2,1)S(1)}, bf16[2,256,256]{2,1,0:T(8,128)(2,1)S(1)}, u32[]{:S(2)}, u32[]{:S(2)}) collective-permute-start(bf16[2,256,256]{2,1,0:T(8,128)(2,1)S(1)} %bitcast.6), channel_id=1, source_target_pairs={{4,8},{8,4},{1,5},{5,1},{6,10},{10,6},{3,7},{7,3},{12,16},{16,12},... | collective-permute-start | bytes 786440 | tf_op jit(solution)/shard_map/ppermute | solution.py:174
  31.9 1.3 %collective-permute-done.1.rest_1_ = bf16[2,256,256]{2,1,0:T(8,128)(2,1)S(1)} collective-permute-done((bf16[2,256,256]{2,1,0:T(8,128)(2,1)S(1)}, bf16[2,256,256]{2,1,0:T(8,128)(2,1)S(1)}, u32[]{:S(2)}, u32[]{:S(2)}) %collective-permute-start.1) | collective-permute-done | bytes 262176 | tf_op jit(solution)/shard_map/ppermute | solution.py:174
  33.1 2.1 %collective-permute-start.3 = (bf16[2,256,256]{2,1,0:T(8,128)(2,1)S(1)}, bf16[2,256,256]{2,1,0:T(8,128)(2,1)S(1)}, u32[]{:S(2)}, u32[]{:S(2)}) collective-permute-start(bf16[2,256,256]{2,1,0:T(8,128)(2,1)S(1)} %collective-permute-done.1.rest_1_), channel_id=1, source_target_pairs={{4,8},{8,4},{1,5},{5,1},{6,10},{10,6},{3,7},{7,3},{12,16},{16,12},... | collective-permute-start | bytes 786440 | tf_op jit(solution)/shard_map/ppermute | solution.py:174
  35.2 2.1 %collective-permute-done.2.rest_2_ = bf16[2,256,256]{2,1,0:T(8,128)(2,1)S(1)} collective-permute-done((bf16[2,256,256]{2,1,0:T(8,128)(2,1)S(1)}, bf16[2,256,256]{2,1,0:T(8,128)(2,1)S(1)}, u32[]{:S(2)}, u32[]{:S(2)}) %collective-permute-start.2) | collective-permute-done | bytes 262176 | tf_op jit(solution)/shard_map/ppermute | solution.py:174
  37.3 1.4 %all-to-all-done.moved_ref = bf16[16,2,16,256]{3,2,1,0:T(8,128)(2,1)S(1)} async-done(((bf16[16,2,16,256]{3,2,1,0:T(8,128)(2,1)}), bf16[16,2,16,256]{3,2,1,0:T(8,128)(2,1)S(1)}, u32[]{:S(2)}, u32[]{:S(2)}) %all-to-all-start) | async-done | bytes 262176 | tf_op jit(solution)/shard_map/all_to_all | solution.py:187
  38.8 9.1 %collective-permute-start.4 = (bf16[2,256,256]{2,1,0:T(8,128)(2,1)S(1)}, bf16[2,256,256]{2,1,0:T(8,128)(2,1)S(1)}, u32[]{:S(2)}, u32[]{:S(2)}) collective-permute-start(bf16[2,256,256]{2,1,0:T(8,128)(2,1)S(1)} %collective-permute-done.2.rest_2_), channel_id=1, source_target_pairs={{0,4},{4,0},{5,9},{9,5},{2,6},{6,2},{7,11},{11,7},{8,12},{12,8},{1... | collective-permute-start | bytes 786440 | tf_op jit(solution)/shard_map/ppermute | solution.py:174
  47.9 0.0 collective-permute-done.3.rest_3_
  47.9 1.9 %collective-permute-start.5 = (bf16[2,256,256]{2,1,0:T(8,128)(2,1)S(1)}, bf16[2,256,256]{2,1,0:T(8,128)(2,1)S(1)}, u32[]{:S(2)}, u32[]{:S(2)}) collective-permute-start(bf16[2,256,256]{2,1,0:T(8,128)(2,1)S(1)} %collective-permute-done.3.rest_3_), channel_id=1, source_target_pairs={{0,4},{4,0},{5,9},{9,5},{2,6},{6,2},{7,11},{11,7},{8,12},{12,8},{1... | collective-permute-start | bytes 786440 | tf_op jit(solution)/shard_map/ppermute | solution.py:174
  49.8 1.8 %collective-permute-done.4.rest_4_ = bf16[2,256,256]{2,1,0:T(8,128)(2,1)S(1)} collective-permute-done((bf16[2,256,256]{2,1,0:T(8,128)(2,1)S(1)}, bf16[2,256,256]{2,1,0:T(8,128)(2,1)S(1)}, u32[]{:S(2)}, u32[]{:S(2)}) %collective-permute-start.4) | collective-permute-done | bytes 262176 | tf_op jit(solution)/shard_map/ppermute | solution.py:174
  51.6 1.9 %collective-permute-start.6 = (bf16[2,256,256]{2,1,0:T(8,128)(2,1)S(1)}, bf16[2,256,256]{2,1,0:T(8,128)(2,1)S(1)}, u32[]{:S(2)}, u32[]{:S(2)}) collective-permute-start(bf16[2,256,256]{2,1,0:T(8,128)(2,1)S(1)} %collective-permute-done.4.rest_4_), channel_id=1, source_target_pairs={{4,8},{8,4},{1,5},{5,1},{6,10},{10,6},{3,7},{7,3},{12,16},{16,12},... | collective-permute-start | bytes 786440 | tf_op jit(solution)/shard_map/ppermute | solution.py:174
  53.5 2.7 %collective-permute-done.5.rest_5_ = bf16[2,256,256]{2,1,0:T(8,128)(2,1)S(1)} collective-permute-done((bf16[2,256,256]{2,1,0:T(8,128)(2,1)S(1)}, bf16[2,256,256]{2,1,0:T(8,128)(2,1)S(1)}, u32[]{:S(2)}, u32[]{:S(2)}) %collective-permute-start.5) | collective-permute-done | bytes 262176 | tf_op jit(solution)/shard_map/ppermute | solution.py:174
  56.2 1.9 %collective-permute-start.7 = (bf16[2,256,256]{2,1,0:T(8,128)(2,1)S(1)}, bf16[2,256,256]{2,1,0:T(8,128)(2,1)S(1)}, u32[]{:S(2)}, u32[]{:S(2)}) collective-permute-start(bf16[2,256,256]{2,1,0:T(8,128)(2,1)S(1)} %collective-permute-done.5.rest_5_), channel_id=1, source_target_pairs={{4,8},{8,4},{1,5},{5,1},{6,10},{10,6},{3,7},{7,3},{12,16},{16,12},... | collective-permute-start | bytes 786440 | tf_op jit(solution)/shard_map/ppermute | solution.py:174
  58.1 0.0 collective-permute-done.lent_ref
  58.1 0.0 copy-start.4
  58.2 3.8 %shard_map.105 = (f32[2,256,256]{2,1,0:T(8,128)S(1)}, bf16[2,256,1024]{2,1,0:T(8,128)(2,1)S(1)}) custom-call(s32[1]{0:T(128)} %bitcast.ch_ref, bf16[256,8192]{1,0:T(8,128)(2,1)} %weight_ref.1, bf16[256,8192]{1,0:T(8,128)(2,1)} %collective-permute-done.lent_ref, bf16[2,256,256]{2,1,0:T(8,128)(2,1)S(1)} %bitcast.7, ...), custom_call_target="tpu_custom_call" | custom-call | flops 805306368 | bytes 8388608 | tf_op jit(solution)/shard_map/pallas_call | solution.py:200
  62.0 0.0 copy-start
  62.0 0.0 copy-start.1
  62.0 0.0 copy-start.2
  62.0 0.0 copy-start.3
  62.0 0.0 collective-permute-done.6.near_ref
  62.1 1.6 %collective-permute-done.7.far_ref = bf16[2,256,256]{2,1,0:T(8,128)(2,1)S(1)} collective-permute-done((bf16[2,256,256]{2,1,0:T(8,128)(2,1)S(1)}, bf16[2,256,256]{2,1,0:T(8,128)(2,1)S(1)}, u32[]{:S(2)}, u32[]{:S(2)}) %collective-permute-start.7) | collective-permute-done | bytes 262176 | tf_op jit(solution)/shard_map/ppermute | solution.py:174
  63.6 0.5 shard_map.106
  64.1 4.8 %all-gather.1 = f32[512,256]{1,0:T(8,128)S(1)} all-gather(f32[256,256]{1,0:T(8,128)S(1)} %get-tuple-element.15), channel_id=3, replica_groups={{0,1},{2,3},{4,5},{6,7},{8,9},{10,11},{12,13},{14,15},{16,17},{18,19},{..., dimensions={0}, use_global_device_ids=true | all-gather | bytes 786432 | tf_op jit(solution)/shard_map/all_gather | solution.py:223
  68.9 13.1 %all_to_all.15.grad_ref = bf16[16,16,256]{2,1,0:T(8,128)(2,1)S(1)} all-to-all(bf16[16,16,256]{2,1,0:T(8,128)(2,1)S(1)} %bitcast.8), channel_id=1, replica_groups=mesh['ctx'=16,'ch'=32] {'ctx'}, dimensions={0} | all-to-all | bytes 262144 | tf_op jit(solution)/shard_map/all_to_all | solution.py:232
  82.0 2.3 %shard_map.108 = bf16[16,2,16,256]{3,2,1,0:T(8,128)(2,1)S(1)} custom-call(bf16[16,16,256]{2,1,0:T(8,128)(2,1)S(1)} %all_to_all.15.grad_ref, bf16[16,2,16,256]{3,2,1,0:T(8,128)(2,1)S(1)} %all-to-all-done.moved_ref, bf16[256,512]{1,0:T(8,128)(2,1)S(1)} %copy-done, bf16[256,512]{1,0:T(8,128)(2,1)S(1)} %copy-done.1, bf16[512,256]{1,0:T(8,128)(2,1)S(1)} %copy-done.2, ...), custom_call_target="tpu_custom_call" | custom-call | tf_op jit(solution)/shard_map/pallas_call | solution.py:233
  84.3 12.7 %all_to_all.16.moved_ref = bf16[16,2,16,256]{3,2,1,0:T(8,128)(2,1)S(1)} all-to-all(bf16[16,2,16,256]{3,2,1,0:T(8,128)(2,1)S(1)} %shard_map.108), channel_id=1, replica_groups=mesh['ctx'=16,'ch'=32] {'ctx'}, dimensions={0} | all-to-all | bytes 524288 | tf_op jit(solution)/shard_map/all_to_all | solution.py:245
  97.0 0.9 shard_map.109
  (6 shorter events, 0.0 us)
Async XLA Ops:
  0.6 57.5 %collective-permute-start = (bf16[256,8192]{1,0:T(8,128)(2,1)}, bf16[256,8192]{1,0:T(8,128)(2,1)}, u32[]{:S(2)}, u32[]{:S(2)}) collective-permute-start(bf16[256,8192]{1,0:T(8,128)(2,1)} %weight_ref.1), channel_id=1, source_target_pairs={{0,1},{1,0},{2,3},{3,2},{4,5},{5,4},{6,7},{7,6},{8,9},{9,8},{10,11... | collective-permute-start | bytes 12582920 | tf_op jit(solution)/shard_map/ppermute | solution.py:174
  16.1 17.0 %collective-permute-start.1 = (bf16[2,256,256]{2,1,0:T(8,128)(2,1)S(1)}, bf16[2,256,256]{2,1,0:T(8,128)(2,1)S(1)}, u32[]{:S(2)}, u32[]{:S(2)}) collective-permute-start(bf16[2,256,256]{2,1,0:T(8,128)(2,1)S(1)} %bitcast.5), channel_id=1, source_target_pairs={{0,2},{2,0},{1,3},{3,1},{4,6},{6,4},{5,7},{7,5},{8,10},{10,8},{9,1... | collective-permute-start | bytes 786440 | tf_op jit(solution)/shard_map/ppermute | solution.py:174
  25.5 13.3 %all-to-all-start = ((bf16[16,2,16,256]{3,2,1,0:T(8,128)(2,1)}), bf16[16,2,16,256]{3,2,1,0:T(8,128)(2,1)S(1)}, u32[]{:S(2)}, u32[]{:S(2)}) async-start(bf16[16,2,16,256]{3,2,1,0:T(8,128)(2,1)} %get-tuple-element.10), calls=%async_computation | async-start | bytes 524288 | tf_op jit(solution)/shard_map/all_to_all | solution.py:187
  29.9 7.4 %collective-permute-start.2 = (bf16[2,256,256]{2,1,0:T(8,128)(2,1)S(1)}, bf16[2,256,256]{2,1,0:T(8,128)(2,1)S(1)}, u32[]{:S(2)}, u32[]{:S(2)}) collective-permute-start(bf16[2,256,256]{2,1,0:T(8,128)(2,1)S(1)} %bitcast.6), channel_id=1, source_target_pairs={{4,8},{8,4},{1,5},{5,1},{6,10},{10,6},{3,7},{7,3},{12,16},{16,12},... | collective-permute-start | bytes 786440 | tf_op jit(solution)/shard_map/ppermute | solution.py:174
  33.1 14.8 %collective-permute-start.3 = (bf16[2,256,256]{2,1,0:T(8,128)(2,1)S(1)}, bf16[2,256,256]{2,1,0:T(8,128)(2,1)S(1)}, u32[]{:S(2)}, u32[]{:S(2)}) collective-permute-start(bf16[2,256,256]{2,1,0:T(8,128)(2,1)S(1)} %collective-permute-done.1.rest_1_), channel_id=1, source_target_pairs={{4,8},{8,4},{1,5},{5,1},{6,10},{10,6},{3,7},{7,3},{12,16},{16,12},... | collective-permute-start | bytes 786440 | tf_op jit(solution)/shard_map/ppermute | solution.py:174
  38.8 12.9 %collective-permute-start.4 = (bf16[2,256,256]{2,1,0:T(8,128)(2,1)S(1)}, bf16[2,256,256]{2,1,0:T(8,128)(2,1)S(1)}, u32[]{:S(2)}, u32[]{:S(2)}) collective-permute-start(bf16[2,256,256]{2,1,0:T(8,128)(2,1)S(1)} %collective-permute-done.2.rest_2_), channel_id=1, source_target_pairs={{0,4},{4,0},{5,9},{9,5},{2,6},{6,2},{7,11},{11,7},{8,12},{12,8},{1... | collective-permute-start | bytes 786440 | tf_op jit(solution)/shard_map/ppermute | solution.py:174
  47.9 8.3 %collective-permute-start.5 = (bf16[2,256,256]{2,1,0:T(8,128)(2,1)S(1)}, bf16[2,256,256]{2,1,0:T(8,128)(2,1)S(1)}, u32[]{:S(2)}, u32[]{:S(2)}) collective-permute-start(bf16[2,256,256]{2,1,0:T(8,128)(2,1)S(1)} %collective-permute-done.3.rest_3_), channel_id=1, source_target_pairs={{0,4},{4,0},{5,9},{9,5},{2,6},{6,2},{7,11},{11,7},{8,12},{12,8},{1... | collective-permute-start | bytes 786440 | tf_op jit(solution)/shard_map/ppermute | solution.py:174
  51.6 10.4 %collective-permute-start.6 = (bf16[2,256,256]{2,1,0:T(8,128)(2,1)S(1)}, bf16[2,256,256]{2,1,0:T(8,128)(2,1)S(1)}, u32[]{:S(2)}, u32[]{:S(2)}) collective-permute-start(bf16[2,256,256]{2,1,0:T(8,128)(2,1)S(1)} %collective-permute-done.4.rest_4_), channel_id=1, source_target_pairs={{4,8},{8,4},{1,5},{5,1},{6,10},{10,6},{3,7},{7,3},{12,16},{16,12},... | collective-permute-start | bytes 786440 | tf_op jit(solution)/shard_map/ppermute | solution.py:174
  56.2 7.4 %collective-permute-start.7 = (bf16[2,256,256]{2,1,0:T(8,128)(2,1)S(1)}, bf16[2,256,256]{2,1,0:T(8,128)(2,1)S(1)}, u32[]{:S(2)}, u32[]{:S(2)}) collective-permute-start(bf16[2,256,256]{2,1,0:T(8,128)(2,1)S(1)} %collective-permute-done.5.rest_5_), channel_id=1, source_target_pairs={{4,8},{8,4},{1,5},{5,1},{6,10},{10,6},{3,7},{7,3},{12,16},{16,12},... | collective-permute-start | bytes 786440 | tf_op jit(solution)/shard_map/ppermute | solution.py:174
  58.1 10.7 %copy-start.4 = (bf16[256,256]{1,0:T(8,128)(2,1)S(1)}, bf16[256,256]{1,0:T(8,128)(2,1)}, u32[]{:S(2)}) copy-start(bf16[256,256]{1,0:T(8,128)(2,1)} %get-tuple-element.16.gate_ref) | copy-start | bytes 393220
  62.0 20.0 %copy-start = (bf16[256,512]{1,0:T(8,128)(2,1)S(1)}, bf16[256,512]{1,0:T(8,128)(2,1)}, u32[]{:S(2)}) copy-start(bf16[256,512]{1,0:T(8,128)(2,1)} %constant.12.clone.high_ref) | copy-start | bytes 786436
  62.0 20.0 %copy-start.1 = (bf16[256,512]{1,0:T(8,128)(2,1)S(1)}, bf16[256,512]{1,0:T(8,128)(2,1)}, u32[]{:S(2)}) copy-start(bf16[256,512]{1,0:T(8,128)(2,1)} %constant.13.clone.low_ref) | copy-start | bytes 786436
  62.0 20.0 %copy-start.2 = (bf16[512,256]{1,0:T(8,128)(2,1)S(1)}, bf16[512,256]{1,0:T(8,128)(2,1)}, u32[]{:S(2)}) copy-start(bf16[512,256]{1,0:T(8,128)(2,1)} %constant.14.clone.ihigh_ref) | copy-start | bytes 786436
  62.0 20.0 %copy-start.3 = (bf16[512,256]{1,0:T(8,128)(2,1)S(1)}, bf16[512,256]{1,0:T(8,128)(2,1)}, u32[]{:S(2)}) copy-start(bf16[512,256]{1,0:T(8,128)(2,1)} %constant.15.clone.ilow_ref) | copy-start | bytes 786436

commit v6 on v4

--- a/solution.py
+++ b/solution.py
@@ -127,14 +127,12 @@
         for which in range(2):
             cross[which, first, :, :block] = totals[2 * which]
             cross[which, first, :, block:] = totals[2 * which + 1]
-    for which in range(2):
-        full = cross[which].reshape(rows, 2 * block)
-        high = full.astype(BF)
-        low = (full - high.astype(F32)).astype(BF)
-        lags = dot(high, ihigh_ref[...]) + dot(high, ilow_ref[...]) + dot(low, ihigh_ref[...])
-        if which == 1:
-            lags = lags * scale
-        out_ref[:, which] = lags.astype(BF).reshape(blocks, lanes, block)
+    full = cross[...].reshape(2 * rows, 2 * block)
+    high = full.astype(BF)
+    low = (full - high.astype(F32)).astype(BF)
+    lags = dot(high, ihigh_ref[...]) + dot(high, ilow_ref[...]) + dot(low, ihigh_ref[...])
+    out_ref[:, 0] = lags[:rows].astype(BF).reshape(blocks, lanes, block)
+    out_ref[:, 1] = (lags[rows:] * scale).astype(BF).reshape(blocks, lanes, block)
 
 
 def finish_kernel(moved_ref, first_ref, second_ref):

time: 98.5 us -> 98.4 us (level)
  no operation moved by 1% of the time
where the time goes in v6:
time: 98.4 us; the launch traced here: 97.8 us
  starting transfers between devices  39.6 us (40%)
  blocking collectives  37.2 us (38%)
  waiting for transfers between devices  10.8 us (11%)
  Pallas kernels  9.34 us (9%)
    ppermute x8, starting transfers between devices, swap(): lax.ppermute(value, 'ch', [(a, b) for pair in pairs for a, b in (pair, pa...  35.1 us
    all_to_all x1, blocking collectives, shards(): lax.all_to_all(gated.reshape(blocks, lanes, block), 'ctx', split_axis=0,...  13.1 us
    all_to_all x1, blocking collectives, shards(): lags = lax.all_to_all(lags, 'ctx', split_axis=0, concat_axis=0, tiled=True)  12.7 us
    ppermute x8, waiting for transfers between devices, swap(): lax.ppermute(value, 'ch', [(a, b) for pair in pairs for a, b in (pair, pa...  9.41 us
    all_gather x1, blocking collectives, shards(): lax.all_gather(out_grad, 'ch', axis=0, tiled=False, axis_index_groups=nei...  6.67 us
    all_gather x1, blocking collectives, shards(): lax.all_gather(lend, 'ch', axis=0, tiled=False, axis_index_groups=cores)  4.76 us
    all_to_all x1, starting transfers between devices, shards(): lax.all_to_all(sequences, 'ctx', split_axis=0, concat_axis=0, tiled=True)  4.47 us
    pallas_call x1, Pallas kernels, shards(): pl.pallas_call(early_kernel, out_shape=[jax.ShapeDtypeStruct((2, channels...  3.82 us
  transfers between devices with their start and end apart: 9, of which 6 were waited for; matrix products, arithmetic and copies ran while one was open for 0% of the time, Pallas kernels for 6%

profile of v6, /device:TPU:1, one launch (start us, length us, event | category | flops | bytes accessed | tf_op | source)
XLA Modules:
  0.0 97.8 jit_solution(14412884522548589615)
XLA Ops:
  0.6 8.8 %collective-permute-start = (bf16[256,8192]{1,0:T(8,128)(2,1)}, bf16[256,8192]{1,0:T(8,128)(2,1)}, u32[]{:S(2)}, u32[]{:S(2)}) collective-permute-start(bf16[256,8192]{1,0:T(8,128)(2,1)} %weight_ref.1), channel_id=1, source_target_pairs={{0,1},{1,0},{2,3},{3,2},{4,5},{5,4},{6,7},{7,6},{8,9},{9,8},{10,11... | collective-permute-start | bytes 12582920 | tf_op jit(solution)/shard_map/ppermute | solution.py:172
  9.4 6.7 %all-gather = bf16[512,256]{1,0:T(8,128)(2,1)S(1)} all-gather(bf16[256,256]{1,0:T(8,128)(2,1)} %param.11), channel_id=2, replica_groups={{0,4},{5,9},{2,6},{7,11},{8,12},{13,17},{10,14},{15,19},{16,20},{21,25}..., dimensions={0}, use_global_device_ids=true | all-gather | bytes 393216 | tf_op jit(solution)/shard_map/all_gather | solution.py:186
  16.1 7.4 %collective-permute-start.1 = (bf16[2,256,256]{2,1,0:T(8,128)(2,1)S(1)}, bf16[2,256,256]{2,1,0:T(8,128)(2,1)S(1)}, u32[]{:S(2)}, u32[]{:S(2)}) collective-permute-start(bf16[2,256,256]{2,1,0:T(8,128)(2,1)S(1)} %bitcast.5), channel_id=1, source_target_pairs={{0,2},{2,0},{1,3},{3,1},{4,6},{6,4},{5,7},{7,5},{8,10},{10,8},{9,1... | collective-permute-start | bytes 786440 | tf_op jit(solution)/shard_map/ppermute | solution.py:172
  23.6 1.9 %shard_map.104 = (bf16[256,256]{1,0:T(8,128)(2,1)}, bf16[16,2,16,256]{3,2,1,0:T(8,128)(2,1)}) custom-call(bf16[256,256]{1,0:T(8,128)(2,1)} %gate_ref.1, bf16[256,256]{1,0:T(8,128)(2,1)} %taps_ref.1, bf16[256,256]{1,0:T(8,128)(2,1)} %input_ref.1), custom_call_target="tpu_custom_call" | custom-call | tf_op jit(solution)/shard_map/pallas_call | solution.py:175
  25.5 4.5 %all-to-all-start = ((bf16[16,2,16,256]{3,2,1,0:T(8,128)(2,1)}), bf16[16,2,16,256]{3,2,1,0:T(8,128)(2,1)S(1)}, u32[]{:S(2)}, u32[]{:S(2)}) async-start(bf16[16,2,16,256]{3,2,1,0:T(8,128)(2,1)} %get-tuple-element.10), calls=%async_computation | async-start | bytes 524288 | tf_op jit(solution)/shard_map/all_to_all | solution.py:185
  29.9 1.9 %collective-permute-start.2 = (bf16[2,256,256]{2,1,0:T(8,128)(2,1)S(1)}, bf16[2,256,256]{2,1,0:T(8,128)(2,1)S(1)}, u32[]{:S(2)}, u32[]{:S(2)}) collective-permute-start(bf16[2,256,256]{2,1,0:T(8,128)(2,1)S(1)} %bitcast.6), channel_id=1, source_target_pairs={{4,8},{8,4},{1,5},{5,1},{6,10},{10,6},{3,7},{7,3},{12,16},{16,12},... | collective-permute-start | bytes 786440 | tf_op jit(solution)/shard_map/ppermute | solution.py:172
  31.9 1.3 %collective-permute-done.1.rest_1_ = bf16[2,256,256]{2,1,0:T(8,128)(2,1)S(1)} collective-permute-done((bf16[2,256,256]{2,1,0:T(8,128)(2,1)S(1)}, bf16[2,256,256]{2,1,0:T(8,128)(2,1)S(1)}, u32[]{:S(2)}, u32[]{:S(2)}) %collective-permute-start.1) | collective-permute-done | bytes 262176 | tf_op jit(solution)/shard_map/ppermute | solution.py:172
  33.1 2.1 %collective-permute-start.3 = (bf16[2,256,256]{2,1,0:T(8,128)(2,1)S(1)}, bf16[2,256,256]{2,1,0:T(8,128)(2,1)S(1)}, u32[]{:S(2)}, u32[]{:S(2)}) collective-permute-start(bf16[2,256,256]{2,1,0:T(8,128)(2,1)S(1)} %collective-permute-done.1.rest_1_), channel_id=1, source_target_pairs={{4,8},{8,4},{1,5},{5,1},{6,10},{10,6},{3,7},{7,3},{12,16},{16,12},... | collective-permute-start | bytes 786440 | tf_op jit(solution)/shard_map/ppermute | solution.py:172
  35.2 2.1 %collective-permute-done.2.rest_2_ = bf16[2,256,256]{2,1,0:T(8,128)(2,1)S(1)} collective-permute-done((bf16[2,256,256]{2,1,0:T(8,128)(2,1)S(1)}, bf16[2,256,256]{2,1,0:T(8,128)(2,1)S(1)}, u32[]{:S(2)}, u32[]{:S(2)}) %collective-permute-start.2) | collective-permute-done | bytes 262176 | tf_op jit(solution)/shard_map/ppermute | solution.py:172
  37.3 1.4 %all-to-all-done.moved_ref = bf16[16,2,16,256]{3,2,1,0:T(8,128)(2,1)S(1)} async-done(((bf16[16,2,16,256]{3,2,1,0:T(8,128)(2,1)}), bf16[16,2,16,256]{3,2,1,0:T(8,128)(2,1)S(1)}, u32[]{:S(2)}, u32[]{:S(2)}) %all-to-all-start) | async-done | bytes 262176 | tf_op jit(solution)/shard_map/all_to_all | solution.py:185
  38.8 9.1 %collective-permute-start.4 = (bf16[2,256,256]{2,1,0:T(8,128)(2,1)S(1)}, bf16[2,256,256]{2,1,0:T(8,128)(2,1)S(1)}, u32[]{:S(2)}, u32[]{:S(2)}) collective-permute-start(bf16[2,256,256]{2,1,0:T(8,128)(2,1)S(1)} %collective-permute-done.2.rest_2_), channel_id=1, source_target_pairs={{0,4},{4,0},{5,9},{9,5},{2,6},{6,2},{7,11},{11,7},{8,12},{12,8},{1... | collective-permute-start | bytes 786440 | tf_op jit(solution)/shard_map/ppermute | solution.py:172
  47.9 0.0 collective-permute-done.3.rest_3_
  47.9 1.9 %collective-permute-start.5 = (bf16[2,256,256]{2,1,0:T(8,128)(2,1)S(1)}, bf16[2,256,256]{2,1,0:T(8,128)(2,1)S(1)}, u32[]{:S(2)}, u32[]{:S(2)}) collective-permute-start(bf16[2,256,256]{2,1,0:T(8,128)(2,1)S(1)} %collective-permute-done.3.rest_3_), channel_id=1, source_target_pairs={{0,4},{4,0},{5,9},{9,5},{2,6},{6,2},{7,11},{11,7},{8,12},{12,8},{1... | collective-permute-start | bytes 786440 | tf_op jit(solution)/shard_map/ppermute | solution.py:172
  49.8 1.8 %collective-permute-done.4.rest_4_ = bf16[2,256,256]{2,1,0:T(8,128)(2,1)S(1)} collective-permute-done((bf16[2,256,256]{2,1,0:T(8,128)(2,1)S(1)}, bf16[2,256,256]{2,1,0:T(8,128)(2,1)S(1)}, u32[]{:S(2)}, u32[]{:S(2)}) %collective-permute-start.4) | collective-permute-done | bytes 262176 | tf_op jit(solution)/shard_map/ppermute | solution.py:172
  51.6 1.9 %collective-permute-start.6 = (bf16[2,256,256]{2,1,0:T(8,128)(2,1)S(1)}, bf16[2,256,256]{2,1,0:T(8,128)(2,1)S(1)}, u32[]{:S(2)}, u32[]{:S(2)}) collective-permute-start(bf16[2,256,256]{2,1,0:T(8,128)(2,1)S(1)} %collective-permute-done.4.rest_4_), channel_id=1, source_target_pairs={{4,8},{8,4},{1,5},{5,1},{6,10},{10,6},{3,7},{7,3},{12,16},{16,12},... | collective-permute-start | bytes 786440 | tf_op jit(solution)/shard_map/ppermute | solution.py:172
  53.5 2.7 %collective-permute-done.5.rest_5_ = bf16[2,256,256]{2,1,0:T(8,128)(2,1)S(1)} collective-permute-done((bf16[2,256,256]{2,1,0:T(8,128)(2,1)S(1)}, bf16[2,256,256]{2,1,0:T(8,128)(2,1)S(1)}, u32[]{:S(2)}, u32[]{:S(2)}) %collective-permute-start.5) | collective-permute-done | bytes 262176 | tf_op jit(solution)/shard_map/ppermute | solution.py:172
  56.2 1.9 %collective-permute-start.7 = (bf16[2,256,256]{2,1,0:T(8,128)(2,1)S(1)}, bf16[2,256,256]{2,1,0:T(8,128)(2,1)S(1)}, u32[]{:S(2)}, u32[]{:S(2)}) collective-permute-start(bf16[2,256,256]{2,1,0:T(8,128)(2,1)S(1)} %collective-permute-done.5.rest_5_), channel_id=1, source_target_pairs={{4,8},{8,4},{1,5},{5,1},{6,10},{10,6},{3,7},{7,3},{12,16},{16,12},... | collective-permute-start | bytes 786440 | tf_op jit(solution)/shard_map/ppermute | solution.py:172
  58.1 0.0 collective-permute-done.lent_ref
  58.1 0.0 copy-start.4
  58.2 3.8 %shard_map.105 = (f32[2,256,256]{2,1,0:T(8,128)S(1)}, bf16[2,256,1024]{2,1,0:T(8,128)(2,1)S(1)}) custom-call(s32[1]{0:T(128)} %bitcast.ch_ref, bf16[256,8192]{1,0:T(8,128)(2,1)} %weight_ref.1, bf16[256,8192]{1,0:T(8,128)(2,1)} %collective-permute-done.lent_ref, bf16[2,256,256]{2,1,0:T(8,128)(2,1)S(1)} %bitcast.7, ...), custom_call_target="tpu_custom_call" | custom-call | flops 805306368 | bytes 8388608 | tf_op jit(solution)/shard_map/pallas_call | solution.py:197
  62.0 0.0 copy-start
  62.0 0.0 copy-start.1
  62.0 0.0 copy-start.2
  62.0 0.0 copy-start.3
  62.0 0.0 collective-permute-done.6.near_ref
  62.1 1.6 %collective-permute-done.7.far_ref = bf16[2,256,256]{2,1,0:T(8,128)(2,1)S(1)} collective-permute-done((bf16[2,256,256]{2,1,0:T(8,128)(2,1)S(1)}, bf16[2,256,256]{2,1,0:T(8,128)(2,1)S(1)}, u32[]{:S(2)}, u32[]{:S(2)}) %collective-permute-start.7) | collective-permute-done | bytes 262176 | tf_op jit(solution)/shard_map/ppermute | solution.py:172
  63.6 0.5 shard_map.106
  64.1 4.8 %all-gather.1 = f32[512,256]{1,0:T(8,128)S(1)} all-gather(f32[256,256]{1,0:T(8,128)S(1)} %get-tuple-element.15), channel_id=3, replica_groups={{0,1},{2,3},{4,5},{6,7},{8,9},{10,11},{12,13},{14,15},{16,17},{18,19},{..., dimensions={0}, use_global_device_ids=true | all-gather | bytes 786432 | tf_op jit(solution)/shard_map/all_gather | solution.py:220
  68.9 13.1 %all_to_all.15.grad_ref = bf16[16,16,256]{2,1,0:T(8,128)(2,1)S(1)} all-to-all(bf16[16,16,256]{2,1,0:T(8,128)(2,1)S(1)} %bitcast.8), channel_id=1, replica_groups=mesh['ctx'=16,'ch'=32] {'ctx'}, dimensions={0} | all-to-all | bytes 262144 | tf_op jit(solution)/shard_map/all_to_all | solution.py:229
  82.0 2.2 %shard_map.108 = bf16[16,2,16,256]{3,2,1,0:T(8,128)(2,1)S(1)} custom-call(bf16[16,16,256]{2,1,0:T(8,128)(2,1)S(1)} %all_to_all.15.grad_ref, bf16[16,2,16,256]{3,2,1,0:T(8,128)(2,1)S(1)} %all-to-all-done.moved_ref, bf16[256,512]{1,0:T(8,128)(2,1)S(1)} %copy-done, bf16[256,512]{1,0:T(8,128)(2,1)S(1)} %copy-done.1, bf16[512,256]{1,0:T(8,128)(2,1)S(1)} %copy-done.2, ...), custom_call_target="tpu_custom_call" | custom-call | tf_op jit(solution)/shard_map/pallas_call | solution.py:230
  84.2 12.7 %all_to_all.16.moved_ref = bf16[16,2,16,256]{3,2,1,0:T(8,128)(2,1)S(1)} all-to-all(bf16[16,2,16,256]{3,2,1,0:T(8,128)(2,1)S(1)} %shard_map.108), channel_id=1, replica_groups=mesh['ctx'=16,'ch'=32] {'ctx'}, dimensions={0} | all-to-all | bytes 524288 | tf_op jit(solution)/shard_map/all_to_all | solution.py:242
  96.9 0.9 shard_map.109
  (6 shorter events, 0.0 us)
Async XLA Ops:
  0.6 57.5 %collective-permute-start = (bf16[256,8192]{1,0:T(8,128)(2,1)}, bf16[256,8192]{1,0:T(8,128)(2,1)}, u32[]{:S(2)}, u32[]{:S(2)}) collective-permute-start(bf16[256,8192]{1,0:T(8,128)(2,1)} %weight_ref.1), channel_id=1, source_target_pairs={{0,1},{1,0},{2,3},{3,2},{4,5},{5,4},{6,7},{7,6},{8,9},{9,8},{10,11... | collective-permute-start | bytes 12582920 | tf_op jit(solution)/shard_map/ppermute | solution.py:172
  16.1 17.0 %collective-permute-start.1 = (bf16[2,256,256]{2,1,0:T(8,128)(2,1)S(1)}, bf16[2,256,256]{2,1,0:T(8,128)(2,1)S(1)}, u32[]{:S(2)}, u32[]{:S(2)}) collective-permute-start(bf16[2,256,256]{2,1,0:T(8,128)(2,1)S(1)} %bitcast.5), channel_id=1, source_target_pairs={{0,2},{2,0},{1,3},{3,1},{4,6},{6,4},{5,7},{7,5},{8,10},{10,8},{9,1... | collective-permute-start | bytes 786440 | tf_op jit(solution)/shard_map/ppermute | solution.py:172
  25.5 13.3 %all-to-all-start = ((bf16[16,2,16,256]{3,2,1,0:T(8,128)(2,1)}), bf16[16,2,16,256]{3,2,1,0:T(8,128)(2,1)S(1)}, u32[]{:S(2)}, u32[]{:S(2)}) async-start(bf16[16,2,16,256]{3,2,1,0:T(8,128)(2,1)} %get-tuple-element.10), calls=%async_computation | async-start | bytes 524288 | tf_op jit(solution)/shard_map/all_to_all | solution.py:185
  29.9 7.4 %collective-permute-start.2 = (bf16[2,256,256]{2,1,0:T(8,128)(2,1)S(1)}, bf16[2,256,256]{2,1,0:T(8,128)(2,1)S(1)}, u32[]{:S(2)}, u32[]{:S(2)}) collective-permute-start(bf16[2,256,256]{2,1,0:T(8,128)(2,1)S(1)} %bitcast.6), channel_id=1, source_target_pairs={{4,8},{8,4},{1,5},{5,1},{6,10},{10,6},{3,7},{7,3},{12,16},{16,12},... | collective-permute-start | bytes 786440 | tf_op jit(solution)/shard_map/ppermute | solution.py:172
  33.1 14.8 %collective-permute-start.3 = (bf16[2,256,256]{2,1,0:T(8,128)(2,1)S(1)}, bf16[2,256,256]{2,1,0:T(8,128)(2,1)S(1)}, u32[]{:S(2)}, u32[]{:S(2)}) collective-permute-start(bf16[2,256,256]{2,1,0:T(8,128)(2,1)S(1)} %collective-permute-done.1.rest_1_), channel_id=1, source_target_pairs={{4,8},{8,4},{1,5},{5,1},{6,10},{10,6},{3,7},{7,3},{12,16},{16,12},... | collective-permute-start | bytes 786440 | tf_op jit(solution)/shard_map/ppermute | solution.py:172
  38.8 12.9 %collective-permute-start.4 = (bf16[2,256,256]{2,1,0:T(8,128)(2,1)S(1)}, bf16[2,256,256]{2,1,0:T(8,128)(2,1)S(1)}, u32[]{:S(2)}, u32[]{:S(2)}) collective-permute-start(bf16[2,256,256]{2,1,0:T(8,128)(2,1)S(1)} %collective-permute-done.2.rest_2_), channel_id=1, source_target_pairs={{0,4},{4,0},{5,9},{9,5},{2,6},{6,2},{7,11},{11,7},{8,12},{12,8},{1... | collective-permute-start | bytes 786440 | tf_op jit(solution)/shard_map/ppermute | solution.py:172
  47.9 8.3 %collective-permute-start.5 = (bf16[2,256,256]{2,1,0:T(8,128)(2,1)S(1)}, bf16[2,256,256]{2,1,0:T(8,128)(2,1)S(1)}, u32[]{:S(2)}, u32[]{:S(2)}) collective-permute-start(bf16[2,256,256]{2,1,0:T(8,128)(2,1)S(1)} %collective-permute-done.3.rest_3_), channel_id=1, source_target_pairs={{0,4},{4,0},{5,9},{9,5},{2,6},{6,2},{7,11},{11,7},{8,12},{12,8},{1... | collective-permute-start | bytes 786440 | tf_op jit(solution)/shard_map/ppermute | solution.py:172
  51.6 10.4 %collective-permute-start.6 = (bf16[2,256,256]{2,1,0:T(8,128)(2,1)S(1)}, bf16[2,256,256]{2,1,0:T(8,128)(2,1)S(1)}, u32[]{:S(2)}, u32[]{:S(2)}) collective-permute-start(bf16[2,256,256]{2,1,0:T(8,128)(2,1)S(1)} %collective-permute-done.4.rest_4_), channel_id=1, source_target_pairs={{4,8},{8,4},{1,5},{5,1},{6,10},{10,6},{3,7},{7,3},{12,16},{16,12},... | collective-permute-start | bytes 786440 | tf_op jit(solution)/shard_map/ppermute | solution.py:172
  56.2 7.4 %collective-permute-start.7 = (bf16[2,256,256]{2,1,0:T(8,128)(2,1)S(1)}, bf16[2,256,256]{2,1,0:T(8,128)(2,1)S(1)}, u32[]{:S(2)}, u32[]{:S(2)}) collective-permute-start(bf16[2,256,256]{2,1,0:T(8,128)(2,1)S(1)} %collective-permute-done.5.rest_5_), channel_id=1, source_target_pairs={{4,8},{8,4},{1,5},{5,1},{6,10},{10,6},{3,7},{7,3},{12,16},{16,12},... | collective-permute-start | bytes 786440 | tf_op jit(solution)/shard_map/ppermute | solution.py:172
  58.1 10.7 %copy-start.4 = (bf16[256,256]{1,0:T(8,128)(2,1)S(1)}, bf16[256,256]{1,0:T(8,128)(2,1)}, u32[]{:S(2)}) copy-start(bf16[256,256]{1,0:T(8,128)(2,1)} %get-tuple-element.16.gate_ref) | copy-start | bytes 393220
  62.0 20.0 %copy-start = (bf16[256,512]{1,0:T(8,128)(2,1)S(1)}, bf16[256,512]{1,0:T(8,128)(2,1)}, u32[]{:S(2)}) copy-start(bf16[256,512]{1,0:T(8,128)(2,1)} %constant.12.clone.high_ref) | copy-start | bytes 786436
  62.0 20.0 %copy-start.1 = (bf16[256,512]{1,0:T(8,128)(2,1)S(1)}, bf16[256,512]{1,0:T(8,128)(2,1)}, u32[]{:S(2)}) copy-start(bf16[256,512]{1,0:T(8,128)(2,1)} %constant.13.clone.low_ref) | copy-start | bytes 786436
  62.0 20.0 %copy-start.2 = (bf16[512,256]{1,0:T(8,128)(2,1)S(1)}, bf16[512,256]{1,0:T(8,128)(2,1)}, u32[]{:S(2)}) copy-start(bf16[512,256]{1,0:T(8,128)(2,1)} %constant.14.clone.ihigh_ref) | copy-start | bytes 786436
  62.0 20.0 %copy-start.3 = (bf16[512,256]{1,0:T(8,128)(2,1)S(1)}, bf16[512,256]{1,0:T(8,128)(2,1)}, u32[]{:S(2)}) copy-start(bf16[512,256]{1,0:T(8,128)(2,1)} %constant.15.clone.ilow_ref) | copy-start | bytes 786436
